TPU v7x, 512 devices: a whole 4x4x16 slice. The times are simulated.
512 devices in a mesh: gx: 32 (over z_hi, x, core), gy: 16 (over y, z_lo).
Axes of the slice: x: 4, y: 4, z: 16 (z_hi: 4, z_lo: 4; z = z_hi * 4 + z_lo), core: 2. Of those that a mesh axis runs over, the one named last changes fastest.
Arguments:
- fields: float32 [8, 512, 512, 128], P(None, 'gx', 'gy'), may hold values from -12 to 12
- displacement: float32 [2, 512, 512], P(None, 'gx', 'gy'), may hold values from -0.3 to 0.3
- donor_tile: int32 [512, 512, 4], P('gx', 'gy'), may hold values from 0 to 31, as said below
- donor_offset: int32 [512, 512, 4], P('gx', 'gy'), may hold values from 0 to 511, as said below
- donor_count: int32 [512, 512], P('gx', 'gy'), may hold values from 1 to 4
Outputs:
- moved_mesh: float32 [2, 512, 512], P(None, 'gx', 'gy')
- remapped: float32 [8, 512, 512, 128], P(None, 'gx', 'gy')
Inputs may be any that keep to these rules, and one draw needn't show every extreme that they name: `donor_tile`: the owning tile lies within one of the new column's own gx index; only slot 0 of a column may name another tile, and of the columns of one tile at most 32 name each neighbouring tile in slot 0, a number reached in every draw. `donor_offset`: the donor lies in the same gy tile as the new column.
All inputs are finite; a program needn't handle non-finite values.
Results may differ from a plain program's by a relative error of at most 0.0001.
Values sent between devices are 32-bit elements; how exact they have to be, the bound alone decides.
No kernel may reach another device: no remote copies, remote signals or barrier semaphores. Data moves between devices by JAX's collectives and lax.ppermute only.
A program may use at most 64 MiB of HBM per device.

v0:
```python
import jax
import jax.numpy as jnp
from jax import lax
from jax.sharding import PartitionSpec as P

DONORS = 4
CAP = 32
SWEEPS = 3
STEPS = 2


BETA_COEF = 0.5
OMEGA_COEF = 0.6
SPREAD_SQ = 64.0


def extended(cells, sides, width):
    for axis, dim in sides:
        count = lax.axis_size(axis)
        ends = count - 1
        head = lax.slice_in_dim(cells, 0, width, axis=dim)
        tail = lax.slice_in_dim(cells, cells.shape[dim] - width, cells.shape[dim], axis=dim)
        cells = jnp.concatenate(
            [
                lax.ppermute(tail, axis, [(i, (i + 1) % count) for i in range(ends)]),
                cells,
                lax.ppermute(head, axis, [((i + 1) % count, i) for i in range(ends)]),
            ],
            axis=dim,
        )
    return cells


def from_behind(block, axis, distance):
    devices = range(lax.axis_size(axis))
    route = [(i - distance, i) for i in devices if i - distance in devices]
    return lax.ppermute(block, axis, route)


def monitor_core(density_pad):
    east_diff = density_pad[2:, 1:-1] - density_pad[:-2, 1:-1]
    north_diff = density_pad[1:-1, 2:] - density_pad[1:-1, :-2]
    steepness = jnp.mean(east_diff * east_diff + north_diff * north_diff, axis=-1)
    return jnp.sqrt(1.0 + BETA_COEF * steepness)


def sweep_core(moved_pad, monitor_pad, interior):
    centre_monitor = monitor_pad[1:-1, 1:-1]
    east_weight = 0.5 * (centre_monitor + monitor_pad[2:, 1:-1])
    west_weight = 0.5 * (centre_monitor + monitor_pad[:-2, 1:-1])
    north_weight = 0.5 * (centre_monitor + monitor_pad[1:-1, 2:])
    south_weight = 0.5 * (centre_monitor + monitor_pad[1:-1, :-2])
    total_weight = east_weight + west_weight + north_weight + south_weight
    blended = (
        east_weight * moved_pad[:, 2:, 1:-1]
        + west_weight * moved_pad[:, :-2, 1:-1]
        + north_weight * moved_pad[:, 1:-1, 2:]
        + south_weight * moved_pad[:, 1:-1, :-2]
    ) / total_weight
    drift = jnp.stack(
        [(east_weight - west_weight) / total_weight, (north_weight - south_weight) / total_weight]
    )
    centre = moved_pad[:, 1:-1, 1:-1]
    relaxed = (1.0 - OMEGA_COEF) * centre + OMEGA_COEF * (blended + drift)
    return jnp.where(interior, relaxed, centre)


def interior_mask(tile_x, tile_y, tile_rows, tile_cols, margin, total_rows, total_cols):
    rows_global = tile_x * tile_rows - margin + jnp.arange(tile_rows + 2 * margin, dtype=jnp.int32)
    cols_global = tile_y * tile_cols - margin + jnp.arange(tile_cols + 2 * margin, dtype=jnp.int32)
    inside_rows = (rows_global >= 1) & (rows_global <= total_rows - 2)
    inside_cols = (cols_global >= 1) & (cols_global <= total_cols - 2)
    return inside_rows[:, None] & inside_cols[None, :]


def relax_mesh(fields, displacement, tile_x, tile_y, total_rows, total_cols):
    tile_rows = displacement.shape[1]
    tile_cols = displacement.shape[2]
    density_pad = extended(fields[0], (("gx", 0), ("gy", 1)), 1)
    monitor = monitor_core(density_pad)
    monitor_pad = extended(monitor, (("gx", 0), ("gy", 1)), 1)
    inner = interior_mask(tile_x, tile_y, tile_rows, tile_cols, 0, total_rows, total_cols)
    moved = displacement
    for sweep_index in range(SWEEPS):
        moved_pad = extended(moved, (("gx", 1), ("gy", 2)), 1)
        moved = sweep_core(moved_pad, monitor_pad, inner)
    return moved


def plan_requests(donor_tile, donor_offset, tile_x):
    tile_cells = donor_tile.shape[0] * donor_tile.shape[1]
    first_owner = donor_tile[:, :, 0].reshape(tile_cells)
    first_place = donor_offset[:, :, 0].reshape(tile_cells)
    to_left = first_owner == tile_x - 1
    to_right = first_owner == tile_x + 1
    left_rank = jnp.cumsum(to_left.astype(jnp.int32)) - 1
    right_rank = jnp.cumsum(to_right.astype(jnp.int32)) - 1
    left_request = (
        jnp.zeros((CAP,), jnp.int32)
        .at[jnp.where(to_left, left_rank, CAP)]
        .set(first_place, mode="drop")
    )
    right_request = (
        jnp.zeros((CAP,), jnp.int32)
        .at[jnp.where(to_right, right_rank, CAP)]
        .set(first_place, mode="drop")
    )
    return (to_left, to_right, left_rank, right_rank, first_place, left_request, right_request)


def remap_local(
    fields,
    old_disp,
    new_disp,
    donor_tile,
    donor_offset,
    donor_count,
    tile_x,
    tile_y,
    routing,
    asked,
):
    field_count, tile_rows, tile_cols, levels = fields.shape
    tile_cells = tile_rows * tile_cols
    column_table = fields.reshape(field_count, tile_cells, levels)
    old_flat = old_disp.reshape(2, tile_cells)
    to_left, to_right, left_rank, right_rank, first_place, left_request, right_request = routing
    asked_by_upper, asked_by_lower = asked
    for_upper = (
        jnp.take(column_table, asked_by_upper, axis=1),
        jnp.take(old_flat, asked_by_upper, axis=1),
    )
    for_lower = (
        jnp.take(column_table, asked_by_lower, axis=1),
        jnp.take(old_flat, asked_by_lower, axis=1),
    )
    from_left_fields, from_left_disp = from_behind((for_upper[0], for_upper[1]), "gx", 1)
    from_right_fields, from_right_disp = from_behind((for_lower[0], for_lower[1]), "gx", -1)
    source_fields = jnp.concatenate([column_table, from_left_fields, from_right_fields], axis=1)
    source_disp = jnp.concatenate([old_flat, from_left_disp, from_right_disp], axis=1)
    first_index = jnp.where(
        to_left,
        tile_cells + left_rank,
        jnp.where(to_right, tile_cells + CAP + right_rank, first_place),
    ).reshape(tile_rows, tile_cols)
    rows_global = (tile_x * tile_rows + jnp.arange(tile_rows, dtype=jnp.int32))[:, None]
    cols_global = (tile_y * tile_cols + jnp.arange(tile_cols, dtype=jnp.int32))[None, :]
    weighted_sum = jnp.zeros((field_count, tile_rows, tile_cols, levels), jnp.float32)
    weight_sum = jnp.zeros((tile_rows, tile_cols), jnp.float32)
    for donor_slot in range(DONORS):
        owner_tile = donor_tile[:, :, donor_slot]
        place = donor_offset[:, :, donor_slot]
        table_index = first_index if donor_slot == 0 else place
        flat_index = table_index.reshape(-1)
        donor_values = jnp.take(source_fields, flat_index, axis=1).reshape(
            field_count, tile_rows, tile_cols, levels
        )
        donor_disp = jnp.take(source_disp, flat_index, axis=1).reshape(2, tile_rows, tile_cols)
        source_row = owner_tile * tile_rows + place // tile_cols
        source_col = tile_y * tile_cols + place % tile_cols
        delta_x = (rows_global - source_row).astype(jnp.float32) + (new_disp[0] - donor_disp[0])
        delta_y = (cols_global - source_col).astype(jnp.float32) + (new_disp[1] - donor_disp[1])
        weight = jnp.where(
            donor_slot < donor_count,
            1.0 / (1.0 + (delta_x * delta_x + delta_y * delta_y) / SPREAD_SQ),
            0.0,
        )
        weighted_sum = weighted_sum + weight[None, :, :, None] * donor_values
        weight_sum = weight_sum + weight
    return weighted_sum / weight_sum[None, :, :, None]


def per_device(fields, displacement, donor_tile, donor_offset, donor_count):
    tile_x = lax.axis_index("gx")
    tile_y = lax.axis_index("gy")
    count_x = lax.axis_size("gx")
    count_y = lax.axis_size("gy")
    total_rows = count_x * displacement.shape[1]
    total_cols = count_y * displacement.shape[2]
    routing = plan_requests(donor_tile, donor_offset, tile_x)
    asked = None
    for step_index in range(STEPS):
        moved = relax_mesh(fields, displacement, tile_x, tile_y, total_rows, total_cols)
        asked = (from_behind(routing[5], "gx", -1), from_behind(routing[6], "gx", 1))
        fields = remap_local(
            fields,
            displacement,
            moved,
            donor_tile,
            donor_offset,
            donor_count,
            tile_x,
            tile_y,
            routing,
            asked,
        )
        displacement = moved
    return (displacement, fields)


def solution(mesh):
    return jax.shard_map(
        per_device,
        mesh=mesh,
        in_specs=(
            P(None, "gx", "gy", None),
            P(None, "gx", "gy"),
            P("gx", "gy", None),
            P("gx", "gy", None),
            P("gx", "gy"),
        ),
        out_specs=(P(None, "gx", "gy"), P(None, "gx", "gy", None)),
        check_vma=False,
    )
```

profile of v0, /device:TPU:111, one launch (start us, length us, event | category | flops | bytes accessed | tf_op | source)
XLA Modules:
  0.0 377.1 jit_solution(13282498399110339350)
XLA Ops:
  4.0 9.0 %collective-permute-start.1 = (f32[1,32,128]{2,1,0:T(8,128)S(1)}, f32[1,32,128]{2,1,0:T(8,128)S(1)}, u32[]{:S(2)}, u32[]{:S(2)}) collective-permute-start(f32[1,32,128]{2,1,0:T(8,128)S(1)} %get-tuple-element.61), channel_id=1, source_target_pairs={{0,16},{16,32},{32,48},{48,64},{64,80},{80,96},{96,112},{112,128},... | collective-permute-start | bytes 49160 | tf_op jit(solution)/shard_map/ppermute | solution.py:25
  15.6 9.7 %collective-permute-start.7 = (f32[2,1,32]{2,1,0:T(1,128)S(1)}, f32[2,1,32]{2,1,0:T(1,128)S(1)}, u32[]{:S(2)}, u32[]{:S(2)}) collective-permute-start(f32[2,1,32]{2,1,0:T(1,128)S(1)} %get-tuple-element.97), channel_id=1, source_target_pairs={{0,16},{16,32},{32,48},{48,64},{64,80},{80,96},{96,112},{112,128},... | collective-permute-start | bytes 776 | tf_op jit(solution)/shard_map/ppermute | solution.py:25
  47.0 9.7 %collective-permute-start.22 = (s32[32]{0:T(128)S(1)}, s32[32]{0:T(128)S(1)}, u32[]{:S(2)}, u32[]{:S(2)}) collective-permute-start(s32[32]{0:T(128)S(1)} %scatter_custom_fusion.1), channel_id=1, source_target_pairs={{0,16},{16,32},{32,48},{48,64},{64,80},{80,96},{96,112},{112,128},... | collective-permute-start | bytes 392 | tf_op jit(solution)/shard_map/ppermute | solution.py:37
  58.0 9.5 %collective-permute-start.24 = (f32[8,32,128]{2,0,1:T(8,128)}, f32[8,32,128]{2,0,1:T(8,128)S(1)}, u32[]{:S(2)}, u32[]{:S(2)}) collective-permute-start(f32[8,32,128]{2,0,1:T(8,128)} %select_bitcast_fusion.11), channel_id=1, source_target_pairs={{0,16},{16,32},{32,48},{48,64},{64,80},{80,96},{96,112},{112,128},... | collective-permute-start | bytes 393224 | tf_op jit(solution)/shard_map/ppermute | solution.py:37
  69.6 6.1 %collective-permute-start.3 = (f32[18,1,128]{2,1,0:T(1,128)S(1)}, f32[18,1,128]{2,1,0:T(1,128)S(1)}, u32[]{:S(2)}, u32[]{:S(2)}) collective-permute-start(f32[18,1,128]{2,1,0:T(1,128)S(1)} %get-tuple-element.66), channel_id=1, source_target_pairs={{0,1},{1,2},{2,3},{3,4},{4,5},{5,6},{6,7},{7,8},{8,9},{9,10},{10,1... | collective-permute-start | bytes 27656 | tf_op jit(solution)/shard_map/ppermute | solution.py:25
  79.8 9.7 %collective-permute-start.6 = (f32[1,32]{1,0:T(1,128)S(1)}, f32[1,32]{1,0:T(1,128)S(1)}, u32[]{:S(2)}, u32[]{:S(2)}) collective-permute-start(f32[1,32]{1,0:T(1,128)S(1)} %get-tuple-element.108), channel_id=1, source_target_pairs={{0,16},{16,32},{32,48},{48,64},{64,80},{80,96},{96,112},{112,128},... | collective-permute-start | bytes 392 | tf_op jit(solution)/shard_map/ppermute | solution.py:25
  106.8 9.7 %collective-permute-start.13 = (f32[2,1,32]{2,1,0:T(1,128)S(1)}, f32[2,1,32]{2,1,0:T(1,128)S(1)}, u32[]{:S(2)}, u32[]{:S(2)}) collective-permute-start(f32[2,1,32]{2,1,0:T(1,128)S(1)} %get-tuple-element.95), channel_id=1, source_target_pairs={{0,16},{16,32},{32,48},{48,64},{64,80},{80,96},{96,112},{112,128},... | collective-permute-start | bytes 776 | tf_op jit(solution)/shard_map/ppermute | solution.py:25
  119.2 6.1 %collective-permute-start.15 = (f32[2,18,1]{2,1,0:T(8,128)S(1)}, f32[2,18,1]{2,1,0:T(8,128)S(1)}, u32[]{:S(2)}, u32[]{:S(2)}) collective-permute-start(f32[2,18,1]{2,1,0:T(8,128)S(1)} %get-tuple-element.84), channel_id=1, source_target_pairs={{0,1},{1,2},{2,3},{3,4},{4,5},{5,6},{6,7},{7,8},{8,9},{9,10},{10,1... | collective-permute-start | bytes 440 | tf_op jit(solution)/shard_map/ppermute | solution.py:25
  128.2 11.3 %collective-permute-start.17 = (f32[2,1,32]{2,1,0:T(1,128)S(1)}, f32[2,1,32]{2,1,0:T(1,128)S(1)}, u32[]{:S(2)}, u32[]{:S(2)}) collective-permute-start(f32[2,1,32]{2,1,0:T(1,128)S(1)} %get-tuple-element.93), channel_id=1, source_target_pairs={{0,16},{16,32},{32,48},{48,64},{64,80},{80,96},{96,112},{112,128},... | collective-permute-start | bytes 776 | tf_op jit(solution)/shard_map/ppermute | solution.py:25
  143.5 6.6 %collective-permute-start.19 = (f32[2,18,1]{2,1,0:T(8,128)S(1)}, f32[2,18,1]{2,1,0:T(8,128)S(1)}, u32[]{:S(2)}, u32[]{:S(2)}) collective-permute-start(f32[2,18,1]{2,1,0:T(8,128)S(1)} %get-tuple-element.82), channel_id=1, source_target_pairs={{0,1},{1,2},{2,3},{3,4},{4,5},{5,6},{6,7},{7,8},{8,9},{9,10},{10,1... | collective-permute-start | bytes 440 | tf_op jit(solution)/shard_map/ppermute | solution.py:25
  153.6 9.6 %collective-permute-start.21 = (f32[2,32]{0,1:T(8,128)S(1)}, f32[2,32]{0,1:T(8,128)S(1)}, u32[]{:S(2)}, u32[]{:S(2)}) collective-permute-start(f32[2,32]{0,1:T(8,128)S(1)} %get-tuple-element.118), channel_id=1, source_target_pairs={{0,16},{16,32},{32,48},{48,64},{64,80},{80,96},{96,112},{112,128},... | collective-permute-start | bytes 776 | tf_op jit(solution)/shard_map/ppermute | solution.py:37
  165.8 9.7 %collective-permute-start.46 = (f32[2,32]{0,1:T(8,128)S(1)}, f32[2,32]{0,1:T(8,128)S(1)}, u32[]{:S(2)}, u32[]{:S(2)}) collective-permute-start(f32[2,32]{0,1:T(8,128)S(1)} %get-tuple-element.117), channel_id=1, source_target_pairs={{0,16},{16,32},{32,48},{48,64},{64,80},{80,96},{96,112},{112,128},... | collective-permute-start | bytes 776 | tf_op jit(solution)/shard_map/ppermute | solution.py:37
  180.5 9.8 %collective-permute-start.33 = (f32[2,1,32]{2,1,0:T(1,128)}, f32[2,1,32]{2,1,0:T(1,128)}, u32[]{:S(2)}, u32[]{:S(2)}) collective-permute-start(f32[2,1,32]{2,1,0:T(1,128)} %get-tuple-element.91), channel_id=1, source_target_pairs={{0,16},{16,32},{32,48},{48,64},{64,80},{80,96},{96,112},{112,128},... | collective-permute-start | bytes 776 | tf_op jit(solution)/shard_map/ppermute | solution.py:25
  216.9 8.6 %fusion.1 = (f32[8,512,128]{2,0,1:T(8,128)S(1)}, f32[512,8,128]{2,1,0:T(8,128)S(1)}, f32[512,8,128]{2,1,0:T(8,128)S(1)}, f32[512,8,128]{2,1,0:T(8,128)S(1)}, f32[512,8,128]{2,1,0:T(8,128)S(1)}) fusion(f32[512]{0:T(512)S(1)} %div.214, f32[512]{0:T(512)S(1)} %mul.541, f32[512]{0:T(512)S(1)} %mul.538, f32[512]{0:T(512)S(1)} %mul.535, f32[512]{0:T(512)S(1)} %mul.532, ...), kind=kLoop, calls=%fused_computation.30 | loop fusion | flops 6291456 | bytes 18886656 | tf_op jit(solution)/shard_map/div | solution.py:170
  230.9 9.7 %collective-permute-start.27 = (f32[1,32,128]{2,1,0:T(8,128)S(1)}, f32[1,32,128]{2,1,0:T(8,128)S(1)}, u32[]{:S(2)}, u32[]{:S(2)}) collective-permute-start(f32[1,32,128]{2,1,0:T(8,128)S(1)} %bitcast.272), channel_id=1, source_target_pairs={{0,16},{16,32},{32,48},{48,64},{64,80},{80,96},{96,112},{112,128},... | collective-permute-start | bytes 49160 | tf_op jit(solution)/shard_map/ppermute | solution.py:25
  243.4 6.1 %collective-permute-start.29 = (f32[18,1,128]{2,1,0:T(1,128)S(1)}, f32[18,1,128]{2,1,0:T(1,128)S(1)}, u32[]{:S(2)}, u32[]{:S(2)}) collective-permute-start(f32[18,1,128]{2,1,0:T(1,128)S(1)} %get-tuple-element.64), channel_id=1, source_target_pairs={{0,1},{1,2},{2,3},{3,4},{4,5},{5,6},{6,7},{7,8},{8,9},{9,10},{10,1... | collective-permute-start | bytes 27656 | tf_op jit(solution)/shard_map/ppermute | solution.py:25
  251.5 6.1 %collective-permute-start.37 = (f32[2,18,1]{2,1,0:T(8,128)S(1)}, f32[2,18,1]{2,1,0:T(8,128)S(1)}, u32[]{:S(2)}, u32[]{:S(2)}) collective-permute-start(f32[2,18,1]{2,1,0:T(8,128)S(1)} %get-tuple-element.80), channel_id=1, source_target_pairs={{0,1},{1,2},{2,3},{3,4},{4,5},{5,6},{6,7},{7,8},{8,9},{9,10},{10,1... | collective-permute-start | bytes 440 | tf_op jit(solution)/shard_map/ppermute | solution.py:25
  260.3 11.3 %collective-permute-start.32 = (f32[1,32]{1,0:T(1,128)S(1)}, f32[1,32]{1,0:T(1,128)S(1)}, u32[]{:S(2)}, u32[]{:S(2)}) collective-permute-start(f32[1,32]{1,0:T(1,128)S(1)} %get-tuple-element.104), channel_id=1, source_target_pairs={{0,16},{16,32},{32,48},{48,64},{64,80},{80,96},{96,112},{112,128},... | collective-permute-start | bytes 392 | tf_op jit(solution)/shard_map/ppermute | solution.py:25
  274.3 6.1 %collective-permute-start.36 = (f32[18,1]{1,0:T(8,128)S(1)}, f32[18,1]{1,0:T(8,128)S(1)}, u32[]{:S(2)}, u32[]{:S(2)}) collective-permute-start(f32[18,1]{1,0:T(8,128)S(1)} %get-tuple-element.99), channel_id=1, source_target_pairs={{0,1},{1,2},{2,3},{3,4},{4,5},{5,6},{6,7},{7,8},{8,9},{9,10},{10,1... | collective-permute-start | bytes 224 | tf_op jit(solution)/shard_map/ppermute | solution.py:25
  284.1 11.3 %collective-permute-start.39 = (f32[2,1,32]{2,1,0:T(1,128)S(1)}, f32[2,1,32]{2,1,0:T(1,128)S(1)}, u32[]{:S(2)}, u32[]{:S(2)}) collective-permute-start(f32[2,1,32]{2,1,0:T(1,128)S(1)} %get-tuple-element.89), channel_id=1, source_target_pairs={{0,16},{16,32},{32,48},{48,64},{64,80},{80,96},{96,112},{112,128},... | collective-permute-start | bytes 776 | tf_op jit(solution)/shard_map/ppermute | solution.py:25
  298.3 6.6 %collective-permute-start.41 = (f32[2,18,1]{2,1,0:T(8,128)S(1)}, f32[2,18,1]{2,1,0:T(8,128)S(1)}, u32[]{:S(2)}, u32[]{:S(2)}) collective-permute-start(f32[2,18,1]{2,1,0:T(8,128)S(1)} %get-tuple-element.78), channel_id=1, source_target_pairs={{0,1},{1,2},{2,3},{3,4},{4,5},{5,6},{6,7},{7,8},{8,9},{9,10},{10,1... | collective-permute-start | bytes 440 | tf_op jit(solution)/shard_map/ppermute | solution.py:25
  304.9 10.3 %collective-permute-start.48 = (f32[8,32,128]{2,0,1:T(8,128)S(1)}, f32[8,32,128]{2,0,1:T(8,128)S(1)}, u32[]{:S(2)}, u32[]{:S(2)}) collective-permute-start(f32[8,32,128]{2,0,1:T(8,128)S(1)} %select_bitcast_fusion.9), channel_id=1, source_target_pairs={{0,16},{16,32},{32,48},{48,64},{64,80},{80,96},{96,112},{112,128},... | collective-permute-start | bytes 393224 | tf_op jit(solution)/shard_map/ppermute | solution.py:37
  317.3 9.7 %collective-permute-start.43 = (f32[2,1,32]{2,1,0:T(1,128)S(1)}, f32[2,1,32]{2,1,0:T(1,128)S(1)}, u32[]{:S(2)}, u32[]{:S(2)}) collective-permute-start(f32[2,1,32]{2,1,0:T(1,128)S(1)} %get-tuple-element.87), channel_id=1, source_target_pairs={{0,16},{16,32},{32,48},{48,64},{64,80},{80,96},{96,112},{112,128},... | collective-permute-start | bytes 776 | tf_op jit(solution)/shard_map/ppermute | solution.py:25
  338.1 15.2 %collective-permute-done.49 = f32[8,32,128]{2,0,1:T(8,128)S(1)} collective-permute-done((f32[8,32,128]{2,0,1:T(8,128)S(1)}, f32[8,32,128]{2,0,1:T(8,128)S(1)}, u32[]{:S(2)}, u32[]{:S(2)}) %collective-permute-start.49) | collective-permute-done | bytes 131104 | tf_op jit(solution)/shard_map/ppermute | solution.py:37
  (294 shorter events, 157.9 us)
Async XLA Ops:
  1.4 66.2 %collective-permute-start = (f32[1,32,128]{2,1,0:T(8,128)S(1)}, f32[1,32,128]{2,1,0:T(8,128)S(1)}, u32[]{:S(2)}, u32[]{:S(2)}) collective-permute-start(f32[1,32,128]{2,1,0:T(8,128)S(1)} %get-tuple-element.62), channel_id=1, source_target_pairs={{16,0},{32,16},{48,32},{64,48},{80,64},{96,80},{112,96},{128,112},... | collective-permute-start | bytes 49160 | tf_op jit(solution)/shard_map/ppermute | solution.py:27
  4.0 63.6 %collective-permute-start.1 = (f32[1,32,128]{2,1,0:T(8,128)S(1)}, f32[1,32,128]{2,1,0:T(8,128)S(1)}, u32[]{:S(2)}, u32[]{:S(2)}) collective-permute-start(f32[1,32,128]{2,1,0:T(8,128)S(1)} %get-tuple-element.61), channel_id=1, source_target_pairs={{0,16},{16,32},{32,48},{48,64},{64,80},{80,96},{96,112},{112,128},... | collective-permute-start | bytes 49160 | tf_op jit(solution)/shard_map/ppermute | solution.py:25
  13.7 53.9 %collective-permute-start.5 = (f32[2,1,32]{2,1,0:T(1,128)S(1)}, f32[2,1,32]{2,1,0:T(1,128)S(1)}, u32[]{:S(2)}, u32[]{:S(2)}) collective-permute-start(f32[2,1,32]{2,1,0:T(1,128)S(1)} %get-tuple-element.98), channel_id=1, source_target_pairs={{16,0},{32,16},{48,32},{64,48},{80,64},{96,80},{112,96},{128,112},... | collective-permute-start | bytes 776 | tf_op jit(solution)/shard_map/ppermute | solution.py:27
  15.6 52.0 %collective-permute-start.7 = (f32[2,1,32]{2,1,0:T(1,128)S(1)}, f32[2,1,32]{2,1,0:T(1,128)S(1)}, u32[]{:S(2)}, u32[]{:S(2)}) collective-permute-start(f32[2,1,32]{2,1,0:T(1,128)S(1)} %get-tuple-element.97), channel_id=1, source_target_pairs={{0,16},{16,32},{32,48},{48,64},{64,80},{80,96},{96,112},{112,128},... | collective-permute-start | bytes 776 | tf_op jit(solution)/shard_map/ppermute | solution.py:25
  31.1 15.9 %collective-permute-start.20 = (s32[32]{0:T(128)S(1)}, s32[32]{0:T(128)S(1)}, u32[]{:S(2)}, u32[]{:S(2)}) collective-permute-start(s32[32]{0:T(128)S(1)} %scatter_custom_fusion), channel_id=1, source_target_pairs={{16,0},{32,16},{48,32},{64,48},{80,64},{96,80},{112,96},{128,112},... | collective-permute-start | bytes 392 | tf_op jit(solution)/shard_map/ppermute | solution.py:37
  58.0 146.3 %collective-permute-start.24 = (f32[8,32,128]{2,0,1:T(8,128)}, f32[8,32,128]{2,0,1:T(8,128)S(1)}, u32[]{:S(2)}, u32[]{:S(2)}) collective-permute-start(f32[8,32,128]{2,0,1:T(8,128)} %select_bitcast_fusion.11), channel_id=1, source_target_pairs={{0,16},{16,32},{32,48},{48,64},{64,80},{80,96},{96,112},{112,128},... | collective-permute-start | bytes 393224 | tf_op jit(solution)/shard_map/ppermute | solution.py:37
  75.7 29.1 %collective-permute-start.11 = (f32[2,18,1]{2,1,0:T(8,128)S(1)}, f32[2,18,1]{2,1,0:T(8,128)S(1)}, u32[]{:S(2)}, u32[]{:S(2)}) collective-permute-start(f32[2,18,1]{2,1,0:T(8,128)S(1)} %get-tuple-element.86), channel_id=1, source_target_pairs={{0,1},{1,2},{2,3},{3,4},{4,5},{5,6},{6,7},{7,8},{8,9},{9,10},{10,1... | collective-permute-start | bytes 440 | tf_op jit(solution)/shard_map/ppermute | solution.py:25
  77.8 15.0 %collective-permute-start.4 = (f32[1,32]{1,0:T(1,128)S(1)}, f32[1,32]{1,0:T(1,128)S(1)}, u32[]{:S(2)}, u32[]{:S(2)}) collective-permute-start(f32[1,32]{1,0:T(1,128)S(1)} %get-tuple-element.107), channel_id=1, source_target_pairs={{16,0},{32,16},{48,32},{64,48},{80,64},{96,80},{112,96},{128,112},... | collective-permute-start | bytes 392 | tf_op jit(solution)/shard_map/ppermute | solution.py:27
  89.4 15.4 %collective-permute-start.9 = (f32[2,18,1]{2,1,0:T(8,128)S(1)}, f32[2,18,1]{2,1,0:T(8,128)S(1)}, u32[]{:S(2)}, u32[]{:S(2)}) collective-permute-start(f32[2,18,1]{2,1,0:T(8,128)S(1)} %get-tuple-element.85), channel_id=1, source_target_pairs={{1,0},{2,1},{3,2},{4,3},{5,4},{6,5},{7,6},{8,7},{9,8},{10,9},{11,1... | collective-permute-start | bytes 440 | tf_op jit(solution)/shard_map/ppermute | solution.py:27
  126.3 15.2 %collective-permute-start.16 = (f32[2,1,32]{2,1,0:T(1,128)S(1)}, f32[2,1,32]{2,1,0:T(1,128)S(1)}, u32[]{:S(2)}, u32[]{:S(2)}) collective-permute-start(f32[2,1,32]{2,1,0:T(1,128)S(1)} %get-tuple-element.94), channel_id=1, source_target_pairs={{16,0},{32,16},{48,32},{64,48},{80,64},{96,80},{112,96},{128,112},... | collective-permute-start | bytes 776 | tf_op jit(solution)/shard_map/ppermute | solution.py:27
  150.1 54.2 %collective-permute-start.25 = (f32[8,32,128]{2,0,1:T(8,128)}, f32[8,32,128]{2,0,1:T(8,128)S(1)}, u32[]{:S(2)}, u32[]{:S(2)}) collective-permute-start(f32[8,32,128]{2,0,1:T(8,128)} %select_bitcast_fusion.10), channel_id=1, source_target_pairs={{16,0},{32,16},{48,32},{64,48},{80,64},{96,80},{112,96},{128,112},... | collective-permute-start | bytes 393224 | tf_op jit(solution)/shard_map/ppermute | solution.py:37
  153.6 21.9 %collective-permute-start.21 = (f32[2,32]{0,1:T(8,128)S(1)}, f32[2,32]{0,1:T(8,128)S(1)}, u32[]{:S(2)}, u32[]{:S(2)}) collective-permute-start(f32[2,32]{0,1:T(8,128)S(1)} %get-tuple-element.118), channel_id=1, source_target_pairs={{0,16},{16,32},{32,48},{48,64},{64,80},{80,96},{96,112},{112,128},... | collective-permute-start | bytes 776 | tf_op jit(solution)/shard_map/ppermute | solution.py:37
  165.8 14.6 %collective-permute-start.46 = (f32[2,32]{0,1:T(8,128)S(1)}, f32[2,32]{0,1:T(8,128)S(1)}, u32[]{:S(2)}, u32[]{:S(2)}) collective-permute-start(f32[2,32]{0,1:T(8,128)S(1)} %get-tuple-element.117), channel_id=1, source_target_pairs={{0,16},{16,32},{32,48},{48,64},{64,80},{80,96},{96,112},{112,128},... | collective-permute-start | bytes 776 | tf_op jit(solution)/shard_map/ppermute | solution.py:37
  175.5 14.8 %collective-permute-start.47 = (f32[2,32]{0,1:T(8,128)S(1)}, f32[2,32]{0,1:T(8,128)}, u32[]{:S(2)}, u32[]{:S(2)}) collective-permute-start(f32[2,32]{0,1:T(8,128)S(1)} %get-tuple-element.119), channel_id=1, source_target_pairs={{16,0},{32,16},{48,32},{64,48},{80,64},{96,80},{112,96},{128,112},... | collective-permute-start | bytes 776 | tf_op jit(solution)/shard_map/ppermute | solution.py:37
  177.5 63.1 %collective-permute-start.31 = (f32[2,1,32]{2,1,0:T(1,128)}, f32[2,1,32]{2,1,0:T(1,128)}, u32[]{:S(2)}, u32[]{:S(2)}) collective-permute-start(f32[2,1,32]{2,1,0:T(1,128)} %get-tuple-element.92), channel_id=1, source_target_pairs={{16,0},{32,16},{48,32},{64,48},{80,64},{96,80},{112,96},{128,112},... | collective-permute-start | bytes 776 | tf_op jit(solution)/shard_map/ppermute | solution.py:27
  180.5 60.1 %collective-permute-start.33 = (f32[2,1,32]{2,1,0:T(1,128)}, f32[2,1,32]{2,1,0:T(1,128)}, u32[]{:S(2)}, u32[]{:S(2)}) collective-permute-start(f32[2,1,32]{2,1,0:T(1,128)} %get-tuple-element.91), channel_id=1, source_target_pairs={{0,16},{16,32},{32,48},{48,64},{64,80},{80,96},{96,112},{112,128},... | collective-permute-start | bytes 776 | tf_op jit(solution)/shard_map/ppermute | solution.py:25
  241.5 16.7 %collective-permute-start.28 = (f32[18,1,128]{2,1,0:T(1,128)S(1)}, f32[18,1,128]{2,1,0:T(1,128)S(1)}, u32[]{:S(2)}, u32[]{:S(2)}) collective-permute-start(f32[18,1,128]{2,1,0:T(1,128)S(1)} %get-tuple-element.63), channel_id=1, source_target_pairs={{1,0},{2,1},{3,2},{4,3},{5,4},{6,5},{7,6},{8,7},{9,8},{10,9},{11,1... | collective-permute-start | bytes 27656 | tf_op jit(solution)/shard_map/ppermute | solution.py:27
  243.4 14.7 %collective-permute-start.29 = (f32[18,1,128]{2,1,0:T(1,128)S(1)}, f32[18,1,128]{2,1,0:T(1,128)S(1)}, u32[]{:S(2)}, u32[]{:S(2)}) collective-permute-start(f32[18,1,128]{2,1,0:T(1,128)S(1)} %get-tuple-element.64), channel_id=1, source_target_pairs={{0,1},{1,2},{2,3},{3,4},{4,5},{5,6},{6,7},{7,8},{8,9},{9,10},{10,1... | collective-permute-start | bytes 27656 | tf_op jit(solution)/shard_map/ppermute | solution.py:25
  249.6 31.8 %collective-permute-start.35 = (f32[2,18,1]{2,1,0:T(8,128)S(1)}, f32[2,18,1]{2,1,0:T(8,128)S(1)}, u32[]{:S(2)}, u32[]{:S(2)}) collective-permute-start(f32[2,18,1]{2,1,0:T(8,128)S(1)} %get-tuple-element.79), channel_id=1, source_target_pairs={{1,0},{2,1},{3,2},{4,3},{5,4},{6,5},{7,6},{8,7},{9,8},{10,9},{11,1... | collective-permute-start | bytes 440 | tf_op jit(solution)/shard_map/ppermute | solution.py:27
  251.5 29.9 %collective-permute-start.37 = (f32[2,18,1]{2,1,0:T(8,128)S(1)}, f32[2,18,1]{2,1,0:T(8,128)S(1)}, u32[]{:S(2)}, u32[]{:S(2)}) collective-permute-start(f32[2,18,1]{2,1,0:T(8,128)S(1)} %get-tuple-element.80), channel_id=1, source_target_pairs={{0,1},{1,2},{2,3},{3,4},{4,5},{5,6},{6,7},{7,8},{8,9},{9,10},{10,1... | collective-permute-start | bytes 440 | tf_op jit(solution)/shard_map/ppermute | solution.py:25
  296.3 18.9 %collective-permute-start.40 = (f32[2,18,1]{2,1,0:T(8,128)S(1)}, f32[2,18,1]{2,1,0:T(8,128)S(1)}, u32[]{:S(2)}, u32[]{:S(2)}) collective-permute-start(f32[2,18,1]{2,1,0:T(8,128)S(1)} %get-tuple-element.77), channel_id=1, source_target_pairs={{1,0},{2,1},{3,2},{4,3},{5,4},{6,5},{7,6},{8,7},{9,8},{10,9},{11,1... | collective-permute-start | bytes 440 | tf_op jit(solution)/shard_map/ppermute | solution.py:27
  298.3 17.0 %collective-permute-start.41 = (f32[2,18,1]{2,1,0:T(8,128)S(1)}, f32[2,18,1]{2,1,0:T(8,128)S(1)}, u32[]{:S(2)}, u32[]{:S(2)}) collective-permute-start(f32[2,18,1]{2,1,0:T(8,128)S(1)} %get-tuple-element.78), channel_id=1, source_target_pairs={{0,1},{1,2},{2,3},{3,4},{4,5},{5,6},{6,7},{7,8},{8,9},{9,10},{10,1... | collective-permute-start | bytes 440 | tf_op jit(solution)/shard_map/ppermute | solution.py:25
  304.9 33.2 %collective-permute-start.48 = (f32[8,32,128]{2,0,1:T(8,128)S(1)}, f32[8,32,128]{2,0,1:T(8,128)S(1)}, u32[]{:S(2)}, u32[]{:S(2)}) collective-permute-start(f32[8,32,128]{2,0,1:T(8,128)S(1)} %select_bitcast_fusion.9), channel_id=1, source_target_pairs={{0,16},{16,32},{32,48},{48,64},{64,80},{80,96},{96,112},{112,128},... | collective-permute-start | bytes 393224 | tf_op jit(solution)/shard_map/ppermute | solution.py:37
  335.7 17.6 %collective-permute-start.49 = (f32[8,32,128]{2,0,1:T(8,128)S(1)}, f32[8,32,128]{2,0,1:T(8,128)S(1)}, u32[]{:S(2)}, u32[]{:S(2)}) collective-permute-start(f32[8,32,128]{2,0,1:T(8,128)S(1)} %select_bitcast_fusion.8), channel_id=1, source_target_pairs={{16,0},{32,16},{48,32},{64,48},{80,64},{96,80},{112,96},{128,112},... | collective-permute-start | bytes 393224 | tf_op jit(solution)/shard_map/ppermute | solution.py:37
  (51 other events, 1126.5 us)
where the time goes:
time: 379 us; the launch traced here: 377 us
  starting transfers between devices  256 us (68%)
  local copies, waits for them, and re-layouts  56 us (15%)
  other arithmetic  40 us (11%)
  waiting for transfers between devices  22.9 us (6%)
    ppermute x20, starting transfers between devices, extended(): lax.ppermute(tail, axis, [(i, (i + 1) % count) for i in range(ends)])  157 us
    ppermute x10, starting transfers between devices, from_behind(): return lax.ppermute(block, axis, route)  58.5 us
    ppermute x20, starting transfers between devices, extended(): lax.ppermute(head, axis, [((i + 1) % count, i) for i in range(ends)])  40.4 us
    gather x8, local copies, waits for them, and re-layouts, remap_local(): jnp.take(source_fields, flat_index, axis=1)  21.5 us
    ppermute x10, waiting for transfers between devices, from_behind(): return lax.ppermute(block, axis, route)  15.2 us
    div x3, other arithmetic, remap_local(): return weighted_sum / weight_sum[None, :, :, None]  14.4 us
    gather x8, local copies, waits for them, and re-layouts, remap_local(): jnp.take(source_disp, flat_index, axis=1).reshape(2, tile_rows, tile_cols)  9.12 us
    select_n x4, other arithmetic, remap_local(): jnp.take(source_fields, flat_index, axis=1)  8.74 us
  transfers between devices with their start and end apart: 50, of which 6 were waited for; matrix products, arithmetic and copies ran while one was open for 19% of the time, Pallas kernels for 0%

commit v1 on v0

v1 whole, which is shorter than its diff:
```python
import jax
import jax.numpy as jnp
from jax import lax
from jax.experimental import pallas as pl
from jax.experimental.pallas import tpu as pltpu
from jax.sharding import PartitionSpec as P

CX = 16
CY = 32
NZ = 128
FIELDS = 8
DONORS = 4
CAP = 32
SWEEPS = 3
STEPS = 2
NX = 512
NY = 512

BETA_COEF = 0.5
OMEGA_COEF = 0.6
SPREAD_SQ = 64.0

TILE = CX * CY
HALO = 4
EXT = CX + 2 * HALO
SIDE = 8
WIDE = CY + 2 * SIDE
HALF = 64
LANES = 128
EDGE = HALO * CY
AT_OFFSETS = EDGE
AT_REST = EDGE + 8
DONOR_ROWS = FIELDS * CAP
REQUEST_MSG = AT_REST + 8
DONOR_MSG = DONOR_ROWS + 8
FULL_MSG = AT_REST + DONOR_MSG
Y_DENSITY = EXT * HALO
Y_MSG = Y_DENSITY + EXT

F32 = jnp.float32
BF16 = jnp.bfloat16
VMEM_BYTES = 56 * 1024 * 1024


def iota(shape, dim):
    return lax.broadcasted_iota(jnp.int32, shape, dim)


def pick(flag, a, b):
    return jnp.where(jnp.full(a.shape, flag, jnp.int32) != 0, a, b)


def widen(x):
    return jnp.concatenate([x, jnp.zeros((x.shape[0], LANES - x.shape[1]), x.dtype)], axis=1)


def spread(x, y):
    gap = jnp.zeros((CX, CY), F32)
    return pltpu.roll(jnp.concatenate([x, gap, y, gap], axis=1), SIDE, 1)


def parities():
    tile_x = lax.axis_index("gx")
    tile_y = lax.axis_index("gy")
    return tile_x, tile_y, lax.rem(tile_x, 2), lax.rem(tile_y, 2)


def first_kernel(disp, head, tail, owner, place, out_even, out_odd, own, aux):
    tile_x, _, px, _ = parities()
    offsets = spread(disp[0], disp[1])
    own[...] = offsets
    first_owner = owner[:, 0, :]
    to_left = widen((first_owner == tile_x - 1).astype(F32))
    to_right = widen((first_owner == tile_x + 1).astype(F32))
    marks = jnp.concatenate([to_left, to_right], axis=0)
    earlier = (iota((LANES, LANES), 0) < iota((LANES, LANES), 1)).astype(F32)
    in_row = jnp.dot(marks, earlier, preferred_element_type=F32)
    totals = jnp.broadcast_to(jnp.sum(marks, axis=1, keepdims=True), (2 * CX, LANES))
    row = lax.rem(iota((2 * CX, LANES), 0), CX)
    before = totals
    for step in (1, 2, 4, 8):
        before = before + jnp.where(row >= step, pltpu.roll(before, step, 0), 0.0)
    rank = in_row + before - totals
    code = jnp.where(
        to_left > 0, rank[:CX], jnp.where(to_right > 0, rank[CX:] + CAP, -1.0)
    )
    aux[:CX, :] = code
    columns = jnp.transpose(jnp.concatenate([code, widen(place[:, 0, :].astype(F32))], axis=0))
    lane = iota((CY, LANES), 1).astype(F32)
    asked = jnp.zeros((CY, LANES), F32)
    for r in range(CX):
        asked = asked + jnp.where(
            columns[:CY, r : r + 1] == lane, columns[:CY, CX + r : CX + r + 1], 0.0
        )
    request = jnp.broadcast_to(jnp.sum(asked, axis=0, keepdims=True), (8, LANES))
    aux[CX:, :] = request
    low, high = head[0], tail[0]
    out_even[:EDGE, :] = pick(px, low, high)
    out_odd[:EDGE, :] = pick(px, high, low)
    low, high = offsets[:8], offsets[8:]
    out_even[AT_OFFSETS:AT_REST, :] = pick(px, low, high)
    out_odd[AT_OFFSETS:AT_REST, :] = pick(px, high, low)
    out_even[AT_REST:, :] = request
    out_odd[AT_REST:, :] = request


def fill_offsets(ext, own, left, right):
    ext[0:HALO, :] = left[HALO:8]
    ext[HALO : HALO + CX, :] = own
    ext[HALO + CX :, :] = right[0:HALO]


def edge_columns(density, from_left, from_right, start):
    parts = []
    for part, rows in ((from_left, HALO), (density, CX), (from_right, HALO)):
        parts.append(part.reshape(rows, CY, NZ)[:, start : start + 8, :])
    return jnp.concatenate(parts, axis=0)


def pack_y(density, halo_even, halo_odd, own, ext, px, py, out_even, out_odd):
    from_left = pick(px, halo_even[:EDGE, :], halo_odd[:EDGE, :])
    from_right = pick(px, halo_odd[:EDGE, :], halo_even[:EDGE, :])
    even = halo_even[AT_OFFSETS:AT_REST, :]
    odd = halo_odd[AT_OFFSETS:AT_REST, :]
    fill_offsets(ext, own, pick(px, even, odd), pick(px, odd, even))
    half = EXT // 2
    low = edge_columns(density, from_left, from_right, 0)
    high = edge_columns(density, from_left, from_right, CY - 8)
    sub = iota((half, 8, NZ), 1)
    low = jnp.where(sub < HALO, low[:half], pltpu.roll(low[half:], HALO, 1))
    high = jnp.where(sub < HALO, pltpu.roll(high[:half], HALO, 1), high[half:])
    low = low.reshape(Y_DENSITY, NZ)
    high = high.reshape(Y_DENSITY, NZ)
    out_even[:Y_DENSITY, :] = pick(py, low, high)
    out_odd[:Y_DENSITY, :] = pick(py, high, low)
    out_even[Y_DENSITY:, :] = ext[...]
    out_odd[Y_DENSITY:, :] = ext[...]


def take_donors(fields, places, out_even, out_odd, start):
    def one(r, carry):
        for out, shift in ((out_even, 0), (out_odd, CAP)):
            p = places[0, r + shift]
            for f in range(FIELDS):
                out[pl.ds(start + f * CAP + r, 1), :] = fields[f, pl.ds(p, 1), :]
        return carry

    lax.fori_loop(0, CAP, one, 0, unroll=8)


def flat_rows(wide):
    row = iota((CX, LANES), 0)
    lane = iota((CX, LANES), 1)
    outs = []
    for base in (SIDE, HALF + SIDE):
        pieces = jnp.zeros((CX, LANES), F32)
        for m in range(4):
            moved = pltpu.roll(wide, (m * CY - base) % LANES, 1)
            pieces = pieces + jnp.where((row % 4 == m) & (lane // CY == m), moved, 0.0)
        quarters = [
            jnp.sum(jnp.where(row // 4 == q, pieces, 0.0), axis=0, keepdims=True) for q in range(4)
        ]
        outs.append(jnp.concatenate(quarters, axis=1))
    return outs


def donor_offsets(own, asked, out_even, out_odd, start):
    flat_x, flat_y = flat_rows(own)
    sub = iota((HALF, LANES), 0)
    lane = iota((HALF, LANES), 1)
    wanted = jnp.sum(
        jnp.where(sub == lane, jnp.broadcast_to(asked, (HALF, LANES)), 0.0), axis=1, keepdims=True
    )
    hit = wanted == iota((HALF, TILE), 1).astype(F32)
    rows = []
    for flat in (flat_x, flat_y):
        column = jnp.sum(jnp.where(hit, flat, 0.0), axis=1, keepdims=True)
        rows.append(jnp.sum(jnp.where(sub == lane, column, 0.0), axis=0, keepdims=True))
    place = iota((8, LANES), 0)
    even = jnp.where(place == 0, rows[0], jnp.where(place == 1, rows[1], 0.0))
    out_even[start : start + 8, :] = even
    out_odd[start : start + 8, :] = pltpu.roll(even, LANES - CAP, 1)


def second_kernel(
    fields, own, halo_even, halo_odd, y_even, y_odd, donor_even, donor_odd, asked_out, ext, places, sem
):
    _, _, px, py = parities()
    lane = iota((8, LANES), 1)
    even = halo_even[AT_REST:, :]
    odd = halo_odd[AT_REST:, :]
    asked = pick(
        px,
        jnp.where(lane < CAP, pltpu.roll(even, LANES - CAP, 1), pltpu.roll(odd, CAP, 1)),
        jnp.where(lane < CAP, even, odd),
    )
    asked_out[...] = asked.astype(jnp.int32)
    copy = pltpu.make_async_copy(asked_out, places, sem)
    copy.start()
    pack_y(fields[0], halo_even, halo_odd, own[...], ext, px, py, y_even, y_odd)
    donor_offsets(own[...], asked[:1], donor_even, donor_odd, DONOR_ROWS)
    copy.wait()
    take_donors(fields, places, donor_even, donor_odd, 0)


def third_kernel(density, own, halo_even, halo_odd, y_even, y_odd, ext):
    _, _, px, py = parities()
    pack_y(density[0], halo_even, halo_odd, own[...], ext, px, py, y_even, y_odd)


def relax(fields, own, halo_even, halo_odd, y_even, y_odd, dens, ext, mon):
    tile_x, tile_y, px, py = parities()
    dens[HALO : HALO + CX, SIDE : SIDE + CY, :] = fields[0].reshape(CX, CY, NZ)
    left = pick(px, halo_even[:EDGE, :], halo_odd[:EDGE, :])
    right = pick(px, halo_odd[:EDGE, :], halo_even[:EDGE, :])
    dens[:HALO, SIDE : SIDE + CY, :] = left.reshape(HALO, CY, NZ)
    dens[HALO + CX :, SIDE : SIDE + CY, :] = right.reshape(HALO, CY, NZ)
    half = EXT // 2
    below = pick(py, y_even[:Y_DENSITY, :], y_odd[:Y_DENSITY, :]).reshape(half, 8, NZ)
    above = pick(py, y_odd[:Y_DENSITY, :], y_even[:Y_DENSITY, :]).reshape(half, 8, NZ)
    dens[:half, :SIDE, :] = pltpu.roll(below, HALO, 1)
    dens[half:, :SIDE, :] = below
    dens[:half, SIDE + CY :, :] = above
    dens[half:, SIDE + CY :, :] = pltpu.roll(above, HALO, 1)

    even = halo_even[AT_OFFSETS:AT_REST, :]
    odd = halo_odd[AT_OFFSETS:AT_REST, :]
    fill_offsets(ext, own, pick(px, even, odd), pick(px, odd, even))
    lane = iota((EXT, LANES), 1)
    half_lane = lax.rem(lane, HALF)
    even = y_even[Y_DENSITY:, :]
    odd = y_odd[Y_DENSITY:, :]
    moved = ext[...]
    moved = jnp.where(half_lane < SIDE, pltpu.roll(pick(py, even, odd), LANES - CY, 1), moved)
    moved = jnp.where(half_lane >= SIDE + CY, pltpu.roll(pick(py, odd, even), CY, 1), moved)

    spot = iota((WIDE, LANES), 0)
    diagonal = spot == lax.rem(iota((WIDE, LANES), 1), HALF)
    mon[0:1, :] = jnp.zeros((1, LANES), F32)
    mon[EXT - 1 :, :] = jnp.zeros((1, LANES), F32)
    for r in range(1, EXT - 1):
        east = dens[r + 1] - dens[r - 1]
        here = dens[r]
        north = pltpu.roll(here, WIDE - 1, 0) - pltpu.roll(here, 1, 0)
        steep = jnp.sum(east * east + north * north, axis=1, keepdims=True)
        mon[r : r + 1, :] = jnp.sum(jnp.where(diagonal, steep, 0.0), axis=0, keepdims=True)
    row_global = tile_x * CX - HALO + iota((EXT, LANES), 0)
    col_global = tile_y * CY - SIDE + half_lane
    on_grid = (row_global >= 0) & (row_global < NX) & (col_global >= 0) & (col_global < NY)
    interior = (
        (row_global >= 1) & (row_global <= NX - 2) & (col_global >= 1) & (col_global <= NY - 2)
    )
    monitor = jnp.where(on_grid, jnp.sqrt(1.0 + (BETA_COEF / NZ) * mon[...]), 0.0)

    def to_east(x):
        return pltpu.roll(x, EXT - 1, 0)

    def to_west(x):
        return pltpu.roll(x, 1, 0)

    def to_north(x):
        return pltpu.roll(x, LANES - 1, 1)

    def to_south(x):
        return pltpu.roll(x, 1, 1)

    east = monitor + to_east(monitor)
    west = monitor + to_west(monitor)
    north = monitor + to_north(monitor)
    south = monitor + to_south(monitor)
    scale = OMEGA_COEF / (east + west + north + south)
    drift = jnp.where(lane < HALF, east - west, north - south) * scale
    east = east * scale
    west = west * scale
    north = north * scale
    south = south * scale
    for _ in range(SWEEPS):
        relaxed = (
            (1.0 - OMEGA_COEF) * moved
            + east * to_east(moved)
            + west * to_west(moved)
            + north * to_north(moved)
            + south * to_south(moved)
            + drift
        )
        moved = jnp.where(interior, relaxed, moved)
    ext[...] = moved
    return ext[HALO : HALO + CX, :]


def weigh(own, moved, owner, place, count, aux, offsets_even, offsets_odd, left_hand, inverse):
    tile_x, _, px, _ = parities()
    flat_x, flat_y = flat_rows(own)
    spot = iota((1, TILE), 1)
    flat_x = flat_x + (spot // CY).astype(F32)
    flat_y = flat_y + lax.rem(spot, CY).astype(F32)

    request = aux[CX : CX + 1, :].astype(jnp.int32)
    lane = iota((1, LANES), 1)
    even, odd = offsets_even, offsets_odd
    left = pick(px, even, odd)
    right = pick(px, odd, even)
    far = jnp.where(iota((8, LANES), 1) < CAP, left, pltpu.roll(right, CAP, 1))
    far_x = far[0:1] + jnp.where(lane < CAP, request // CY - CX, request // CY + CX).astype(F32)
    far_y = far[1:2] + lax.rem(request, CY).astype(F32)
    far_x = jnp.where(lane < HALF, far_x, pltpu.roll(far_x, HALF, 1))
    far_y = jnp.where(lane < HALF, far_y, pltpu.roll(far_y, HALF, 1))
    far_lane = lax.rem(lane, HALF).astype(F32)
    near_half = iota((CY, LANES), 1) < HALF

    live = count[...]
    codes = []
    for k in range(DONORS):
        here = owner[:, k, :] == tile_x
        codes.append(widen(jnp.where(here & (k < live), place[:, k, :], -1).astype(F32)))
    codes.append(jnp.where(widen(live.astype(F32)) > 0, aux[:CX, :], -1.0))
    columns = jnp.transpose(jnp.concatenate(codes, axis=0))
    shifts = jnp.transpose(moved)
    along = iota((CY, 1), 0).astype(F32)
    spots = iota((CY, TILE), 1).astype(F32)

    def weight(dx, dy):
        bulk = SPREAD_SQ + dx * dx + dy * dy
        guess = pl.reciprocal(bulk, approx=True)
        return guess * (2.0 - bulk * guess)

    for r in range(CX):
        at_x = shifts[SIDE : SIDE + CY, r : r + 1] + float(r)
        at_y = shifts[HALF + SIDE : HALF + SIDE + CY, r : r + 1] + along
        dense = weight(at_x - flat_x, at_y - flat_y)
        total = jnp.zeros((CY, TILE), F32)
        for k in range(DONORS):
            code = columns[:CY, k * CX + r : k * CX + r + 1]
            total = total + jnp.where(code == spots, dense, 0.0)
        code = columns[:CY, DONORS * CX + r : DONORS * CX + r + 1]
        remote = jnp.where(code == far_lane, weight(at_x - far_x, at_y - far_y), 0.0)
        norm = jnp.sum(total, axis=1, keepdims=True) + jnp.sum(
            jnp.where(near_half, remote, 0.0), axis=1, keepdims=True
        )
        rows = slice(r * CY, (r + 1) * CY)
        inverse[rows, :] = jnp.broadcast_to(1.0 / norm, (CY, LANES))
        high = total.astype(BF16)
        left_hand[rows, 0:TILE] = high
        left_hand[rows, TILE : 2 * TILE] = (total - high.astype(F32)).astype(BF16)
        left_hand[rows, 2 * TILE : 3 * TILE] = high
        high = remote.astype(BF16)
        low = (remote - high.astype(F32)).astype(BF16)
        base = 3 * TILE
        left_hand[rows, base : base + LANES] = jnp.where(near_half, high.astype(F32), low.astype(F32)).astype(BF16)
        left_hand[rows, base + LANES : base + 2 * LANES] = jnp.where(near_half, high.astype(F32), 0.0).astype(BF16)


def split(x):
    high = x.astype(BF16)
    return high, (x - high.astype(F32)).astype(BF16)


def combine(fields, donors_even, donors_odd, px, left_hand, right_hand, inverse, out):
    for f in range(FIELDS):
        n, lanes = f // 2, slice((f % 2) * NZ, (f % 2) * NZ + NZ)
        high, low = split(fields[f])
        right_hand[n, 0:TILE, lanes] = high
        right_hand[n, TILE : 2 * TILE, lanes] = high
        right_hand[n, 2 * TILE : 3 * TILE, lanes] = low
        even = donors_even(f)
        odd = donors_odd(f)
        both = jnp.concatenate([pick(px, even, odd), pick(px, odd, even)], axis=0)
        high, low = split(both)
        base = 3 * TILE
        right_hand[n, base : base + HALF, lanes] = high
        right_hand[n, base + HALF : base + 2 * HALF, lanes] = high
        right_hand[n, base + 2 * HALF : base + 3 * HALF, lanes] = low
        right_hand[n, base + 3 * HALF : base + 4 * HALF, lanes] = jnp.zeros((HALF, NZ), BF16)

    for n in range(FIELDS // 2):
        mixed = jnp.dot(left_hand[...], right_hand[n], preferred_element_type=F32)
        out[2 * n] = mixed[:, :NZ] * inverse[...]
        out[2 * n + 1] = mixed[:, NZ:] * inverse[...]


def step_kernel(
    fields, own, halo_even, halo_odd, y_even, y_odd, donor_even, donor_odd, owner, place, count, aux, asked,
    out, own_out, x_even, x_odd,
    dens, ext, mon, left_hand, right_hand, inverse, places, sem,
):
    _, _, px, _ = parities()
    copy = pltpu.make_async_copy(asked, places, sem)
    copy.start()
    moved = relax(fields, own[...], halo_even, halo_odd, y_even, y_odd, dens, ext, mon)
    own_out[...] = moved
    weigh(
        own[...], moved, owner, place, count, aux,
        donor_even[DONOR_ROWS:, :], donor_odd[DONOR_ROWS:, :], left_hand, inverse,
    )
    combine(
        fields,
        lambda f: donor_even[f * CAP : (f + 1) * CAP, :],
        lambda f: donor_odd[f * CAP : (f + 1) * CAP, :],
        px, left_hand, right_hand, inverse, out,
    )
    low, high = out[0, :EDGE, :], out[0, TILE - EDGE :, :]
    x_even[:EDGE, :] = pick(px, low, high)
    x_odd[:EDGE, :] = pick(px, high, low)
    low, high = moved[:8], moved[8:]
    x_even[AT_OFFSETS:AT_REST, :] = pick(px, low, high)
    x_odd[AT_OFFSETS:AT_REST, :] = pick(px, high, low)
    donor_offsets(moved, asked[:1, :].astype(F32), x_even, x_odd, AT_REST + DONOR_ROWS)
    copy.wait()
    take_donors(out, places, x_even, x_odd, AT_REST)


def last_kernel(
    fields, own, x_even, x_odd, y_even, y_odd, owner, place, count, aux,
    moved_out, out,
    dens, ext, mon, left_hand, right_hand, inverse,
):
    _, _, px, _ = parities()
    moved = relax(fields, own[...], x_even, x_odd, y_even, y_odd, dens, ext, mon)
    moved_out[0] = pltpu.roll(moved, LANES - SIDE, 1)[:, :CY]
    moved_out[1] = pltpu.roll(moved, HALF - SIDE, 1)[:, :CY]
    at = AT_REST + DONOR_ROWS
    weigh(
        own[...], moved, owner, place, count, aux,
        x_even[at : at + 8, :], x_odd[at : at + 8, :], left_hand, inverse,
    )
    combine(
        fields,
        lambda f: x_even[AT_REST + f * CAP : AT_REST + (f + 1) * CAP, :],
        lambda f: x_odd[AT_REST + f * CAP : AT_REST + (f + 1) * CAP, :],
        px, left_hand, right_hand, inverse, out,
    )


def shape(*dims, dtype=F32):
    return jax.ShapeDtypeStruct(dims, dtype)


def call(kernel, outs, scratch=(), in_specs=None, name=None):
    extra = {} if in_specs is None else {"in_specs": in_specs, "grid": (1,)}
    return pl.pallas_call(
        kernel,
        out_shape=outs,
        scratch_shapes=list(scratch),
        compiler_params=pltpu.CompilerParams(vmem_limit_bytes=VMEM_BYTES),
        name=name,
        **extra,
    )


def swap_pairs(block, axis, odd):
    count = lax.axis_size(axis)
    route = []
    for a in range(1 if odd else 0, count - 1, 2):
        route += [(a, a + 1), (a + 1, a)]
    return lax.ppermute(block, axis, route)


def swap(even, odd, axis):
    return swap_pairs(even, axis, False), swap_pairs(odd, axis, True)


WORK = (
    pltpu.VMEM((EXT, WIDE, NZ), F32),
    pltpu.VMEM((EXT, LANES), F32),
    pltpu.VMEM((EXT, LANES), F32),
    pltpu.VMEM((TILE, 3 * TILE + 4 * HALF), BF16),
    pltpu.VMEM((FIELDS // 2, 3 * TILE + 4 * HALF, 2 * NZ), BF16),
    pltpu.VMEM((TILE, LANES), F32),
)
PLACES = (pltpu.SMEM((8, LANES), jnp.int32), pltpu.SemaphoreType.DMA)


def whole():
    return pl.BlockSpec(memory_space=pltpu.VMEM)


def density_rows(start, rows):
    return pl.BlockSpec((1, rows, NZ), lambda i: (0, start // rows, 0))


def per_device(fields, displacement, donor_tile, donor_offset, donor_count):
    fields = fields.reshape(FIELDS, TILE, NZ)
    owner = donor_tile.transpose(0, 2, 1)
    place = donor_offset.transpose(0, 2, 1)
    even, odd, own, aux = call(
        first_kernel,
        (shape(REQUEST_MSG, LANES), shape(REQUEST_MSG, LANES), shape(CX, LANES), shape(CX + 8, LANES)),
        in_specs=[whole(), density_rows(0, EDGE), density_rows(TILE - EDGE, EDGE), whole(), whole()],
        name="pack_first",
    )(displacement, fields, fields, owner, place)
    halo = swap(even, odd, "gx")
    y_even, y_odd, d_even, d_odd, asked = call(
        second_kernel,
        (
            shape(Y_MSG, LANES), shape(Y_MSG, LANES), shape(DONOR_MSG, LANES), shape(DONOR_MSG, LANES),
            shape(8, LANES, dtype=jnp.int32),
        ),
        scratch=(pltpu.VMEM((EXT, LANES), F32),) + PLACES,
        name="pack_donors",
    )(fields, own, *halo)
    y_halo = swap(y_even, y_odd, "gy")
    donors = swap(d_even, d_odd, "gx")
    fields, own, even, odd = call(
        step_kernel,
        (shape(FIELDS, TILE, NZ), shape(CX, LANES), shape(FULL_MSG, LANES), shape(FULL_MSG, LANES)),
        scratch=WORK + PLACES,
        name="step_one",
    )(fields, own, *halo, *y_halo, *donors, owner, place, donor_count, aux, asked)
    halo = swap(even, odd, "gx")
    y_even, y_odd = call(
        third_kernel,
        (shape(Y_MSG, LANES), shape(Y_MSG, LANES)),
        scratch=(pltpu.VMEM((EXT, LANES), F32),),
        in_specs=[density_rows(0, TILE), whole(), whole(), whole()],
        name="pack_y",
    )(fields, own, *halo)
    y_halo = swap(y_even, y_odd, "gy")
    moved, fields = call(
        last_kernel,
        (shape(2, CX, CY), shape(FIELDS, TILE, NZ)),
        scratch=WORK,
        name="step_two",
    )(fields, own, *halo, *y_halo, owner, place, donor_count, aux)
    return moved, fields.reshape(FIELDS, CX, CY, NZ)


def solution(mesh):
    return jax.shard_map(
        per_device,
        mesh=mesh,
        in_specs=(
            P(None, "gx", "gy", None),
            P(None, "gx", "gy"),
            P("gx", "gy", None),
            P("gx", "gy", None),
            P("gx", "gy"),
        ),
        out_specs=(P(None, "gx", "gy"), P(None, "gx", "gy", None)),
        check_vma=False,
    )
```

time: 379 us -> 94.9 us (0.25)
  the two profiles are of different devices: /device:TPU:111 before, /device:TPU:480 now
where the time goes in v1:
time: 94.9 us; the launch traced here: 94.3 us
  starting transfers between devices  42.6 us (45%)
  waiting for transfers between devices  26.2 us (28%)
  Pallas kernels  22.1 us (23%)
  local copies, waits for them, and re-layouts  2.65 us (3%)
    ppermute x10, starting transfers between devices, swap_pairs(): return lax.ppermute(block, axis, route)  42.6 us
    ppermute x10, waiting for transfers between devices, swap_pairs(): return lax.ppermute(block, axis, route)  26.2 us
    pallas_call x1, Pallas kernels, per_device(): call(step_kernel, (shape(FIELDS, TILE, NZ), shape(CX, LANES), shape(FULL_...  7.71 us
    pallas_call x1, Pallas kernels, per_device(): call(last_kernel, (shape(2, CX, CY), shape(FIELDS, TILE, NZ)), scratch=WO...  7.19 us
    pallas_call x1, Pallas kernels, per_device(): call(second_kernel, (shape(Y_MSG, LANES), shape(Y_MSG, LANES), shape(DONO...  3.32 us
    unnamed x20, local copies, waits for them, and re-layouts  2.65 us
    pallas_call x1, Pallas kernels, per_device(): call(first_kernel, (shape(REQUEST_MSG, LANES), shape(REQUEST_MSG, LANES),...  2.09 us
  transfers between devices with their start and end apart: 10, of which 4 were waited for; matrix products, arithmetic and copies ran while one was open for 0% of the time, Pallas kernels for 0%

profile of v1, /device:TPU:480, one launch (start us, length us, event | category | flops | bytes accessed | tf_op | source)
XLA Modules:
  0.0 94.3 jit_solution(7916165820735249695)
XLA Ops:
  0.6 2.1 %pack_first.1 = (f32[144,128]{1,0:T(8,128)}, f32[144,128]{1,0:T(8,128)}, f32[16,128]{1,0:T(8,128)}, f32[24,128]{1,0:T(8,128)}) custom-call(f32[2,16,32]{2,1,0:T(8,128)} %disp.1, f32[8,512,128]{2,1,0:T(8,128)} %bitcast.4, f32[8,512,128]{2,1,0:T(8,128)} %bitcast.5, s32[16,4,32]{2,1,0:T(4,128)} %bitcast.8, s32[16,4,32]{2,1,0:T(4,128)} %bitcast.11), custom_call_target="tpu_custom_call" | custom-call | tf_op jit(solution)/shard_map/pack_first/pallas_call | solution.py:485
  2.7 1.9 %collective-permute-start = (f32[144,128]{1,0:T(8,128)}, f32[144,128]{1,0:T(8,128)S(1)}, u32[]{:S(2)}, u32[]{:S(2)}) collective-permute-start(f32[144,128]{1,0:T(8,128)} %get-tuple-element.20), channel_id=1, source_target_pairs={{0,16},{16,0},{32,48},{48,32},{64,80},{80,64},{96,112},{112,96},{1... | collective-permute-start | bytes 221192 | tf_op jit(solution)/shard_map/ppermute | solution.py:455
  4.6 7.8 %collective-permute-start.1 = (f32[144,128]{1,0:T(8,128)}, f32[144,128]{1,0:T(8,128)S(1)}, u32[]{:S(2)}, u32[]{:S(2)}) collective-permute-start(f32[144,128]{1,0:T(8,128)} %get-tuple-element.21), channel_id=1, source_target_pairs={{16,32},{32,16},{48,64},{64,48},{80,96},{96,80},{112,128},{128,112... | collective-permute-start | bytes 221192 | tf_op jit(solution)/shard_map/ppermute | solution.py:455
  12.4 6.5 %collective-permute-done.1.halo_odd = f32[144,128]{1,0:T(8,128)S(1)} collective-permute-done((f32[144,128]{1,0:T(8,128)}, f32[144,128]{1,0:T(8,128)S(1)}, u32[]{:S(2)}, u32[]{:S(2)}) %collective-permute-start.1) | collective-permute-done | bytes 73760 | tf_op jit(solution)/shard_map/ppermute | solution.py:455
  18.9 0.6 copy-done.3
  19.5 3.3 %pack_donors.1 = (f32[120,128]{1,0:T(8,128)}, f32[120,128]{1,0:T(8,128)}, f32[264,128]{1,0:T(8,128)}, f32[264,128]{1,0:T(8,128)}, s32[8,128]{1,0:T(8,128)}) custom-call(f32[8,512,128]{2,1,0:T(8,128)} %bitcast.6, f32[16,128]{1,0:T(8,128)} %get-tuple-element.19.own, f32[144,128]{1,0:T(8,128)} %copy-done.2, f32[144,128]{1,0:T(8,128)} %copy-done.3), custom_call_target="tpu_custom_call" | custom-call | tf_op jit(solution)/shard_map/pack_donors/pallas_call | solution.py:492
  22.9 1.9 %collective-permute-start.4 = (f32[264,128]{1,0:T(8,128)}, f32[264,128]{1,0:T(8,128)S(1)}, u32[]{:S(2)}, u32[]{:S(2)}) collective-permute-start(f32[264,128]{1,0:T(8,128)} %get-tuple-element.24), channel_id=1, source_target_pairs={{0,16},{16,0},{32,48},{48,32},{64,80},{80,64},{96,112},{112,96},{1... | collective-permute-start | bytes 405512 | tf_op jit(solution)/shard_map/ppermute | solution.py:455
  24.8 5.7 %collective-permute-start.5 = (f32[264,128]{1,0:T(8,128)}, f32[264,128]{1,0:T(8,128)S(1)}, u32[]{:S(2)}, u32[]{:S(2)}) collective-permute-start(f32[264,128]{1,0:T(8,128)} %get-tuple-element.25), channel_id=1, source_target_pairs={{16,32},{32,16},{48,64},{64,48},{80,96},{96,80},{112,128},{128,112... | collective-permute-start | bytes 405512 | tf_op jit(solution)/shard_map/ppermute | solution.py:455
  30.5 3.6 %collective-permute-start.2 = (f32[120,128]{1,0:T(8,128)}, f32[120,128]{1,0:T(8,128)S(1)}, u32[]{:S(2)}, u32[]{:S(2)}) collective-permute-start(f32[120,128]{1,0:T(8,128)} %get-tuple-element.22), channel_id=1, source_target_pairs={{0,1},{1,0},{2,3},{3,2},{4,5},{5,4},{6,7},{7,6},{8,9},{9,8},{10,11... | collective-permute-start | bytes 184328 | tf_op jit(solution)/shard_map/ppermute | solution.py:455
  34.1 5.5 %collective-permute-start.3 = (f32[120,128]{1,0:T(8,128)}, f32[120,128]{1,0:T(8,128)S(1)}, u32[]{:S(2)}, u32[]{:S(2)}) collective-permute-start(f32[120,128]{1,0:T(8,128)} %get-tuple-element.23), channel_id=1, source_target_pairs={{1,2},{2,1},{3,4},{4,3},{5,6},{6,5},{7,8},{8,7},{9,10},{10,9},{11,... | collective-permute-start | bytes 184328 | tf_op jit(solution)/shard_map/ppermute | solution.py:455
  39.6 3.5 %collective-permute-done.3.y_odd = f32[120,128]{1,0:T(8,128)S(1)} collective-permute-done((f32[120,128]{1,0:T(8,128)}, f32[120,128]{1,0:T(8,128)S(1)}, u32[]{:S(2)}, u32[]{:S(2)}) %collective-permute-start.3) | collective-permute-done | bytes 61472 | tf_op jit(solution)/shard_map/ppermute | solution.py:455
  43.2 0.6 copy-done.7
  43.7 0.1 copy-done.4
  43.9 7.7 %step_one.1 = (f32[8,512,128]{2,1,0:T(8,128)}, f32[16,128]{1,0:T(8,128)}, f32[400,128]{1,0:T(8,128)}, f32[400,128]{1,0:T(8,128)}) custom-call(f32[8,512,128]{2,1,0:T(8,128)} %bitcast.7, f32[16,128]{1,0:T(8,128)} %get-tuple-element.19.own, f32[144,128]{1,0:T(8,128)} %copy-done.2, f32[144,128]{1,0:T(8,128)} %copy-done.3, f32[120,128]{1,0:T(8,128)} %copy-done.6, ...), custom_call_target="tpu_custom_call" | custom-call | tf_op jit(solution)/shard_map/step_one/pallas_call | solution.py:503
  51.6 1.9 %collective-permute-start.6 = (f32[400,128]{1,0:T(8,128)}, f32[400,128]{1,0:T(8,128)S(1)}, u32[]{:S(2)}, u32[]{:S(2)}) collective-permute-start(f32[400,128]{1,0:T(8,128)} %get-tuple-element.30), channel_id=1, source_target_pairs={{0,16},{16,0},{32,48},{48,32},{64,80},{80,64},{96,112},{112,96},{1... | collective-permute-start | bytes 614408 | tf_op jit(solution)/shard_map/ppermute | solution.py:455
  53.5 3.2 %collective-permute-start.7 = (f32[400,128]{1,0:T(8,128)}, f32[400,128]{1,0:T(8,128)S(1)}, u32[]{:S(2)}, u32[]{:S(2)}) collective-permute-start(f32[400,128]{1,0:T(8,128)} %get-tuple-element.31), channel_id=1, source_target_pairs={{16,32},{32,16},{48,64},{64,48},{80,96},{96,80},{112,128},{128,112... | collective-permute-start | bytes 614408 | tf_op jit(solution)/shard_map/ppermute | solution.py:455
  56.7 10.9 %collective-permute-done.7.halo_odd.x_odd = f32[400,128]{1,0:T(8,128)S(1)} collective-permute-done((f32[400,128]{1,0:T(8,128)}, f32[400,128]{1,0:T(8,128)S(1)}, u32[]{:S(2)}, u32[]{:S(2)}) %collective-permute-start.7) | collective-permute-done | bytes 204832 | tf_op jit(solution)/shard_map/ppermute | solution.py:455
  67.6 0.7 copy-done.1
  68.3 1.8 %pack_y.1 = (f32[120,128]{1,0:T(8,128)}, f32[120,128]{1,0:T(8,128)}) custom-call(f32[8,512,128]{2,1,0:T(8,128)} %get-tuple-element.28.density.fields, f32[16,128]{1,0:T(8,128)} %get-tuple-element.29.own, f32[400,128]{1,0:T(8,128)} %copy-done, f32[400,128]{1,0:T(8,128)} %copy-done.1), custom_call_target="tpu_custom_call" | custom-call | tf_op jit(solution)/shard_map/pack_y/pallas_call | solution.py:510
  70.1 7.4 %collective-permute-start.8 = (f32[120,128]{1,0:T(8,128)}, f32[120,128]{1,0:T(8,128)S(1)}, u32[]{:S(2)}, u32[]{:S(2)}) collective-permute-start(f32[120,128]{1,0:T(8,128)} %get-tuple-element.32), channel_id=1, source_target_pairs={{0,1},{1,0},{2,3},{3,2},{4,5},{5,4},{6,7},{7,6},{8,9},{9,8},{10,11... | collective-permute-start | bytes 184328 | tf_op jit(solution)/shard_map/ppermute | solution.py:455
  77.5 3.7 %collective-permute-start.9 = (f32[120,128]{1,0:T(8,128)}, f32[120,128]{1,0:T(8,128)S(1)}, u32[]{:S(2)}, u32[]{:S(2)}) collective-permute-start(f32[120,128]{1,0:T(8,128)} %get-tuple-element.33), channel_id=1, source_target_pairs={{1,2},{2,1},{3,4},{4,3},{5,6},{6,5},{7,8},{8,7},{9,10},{10,9},{11,... | collective-permute-start | bytes 184328 | tf_op jit(solution)/shard_map/ppermute | solution.py:455
  81.2 5.3 %collective-permute-done.9.y_odd = f32[120,128]{1,0:T(8,128)S(1)} collective-permute-done((f32[120,128]{1,0:T(8,128)}, f32[120,128]{1,0:T(8,128)S(1)}, u32[]{:S(2)}, u32[]{:S(2)}) %collective-permute-start.9) | collective-permute-done | bytes 61472 | tf_op jit(solution)/shard_map/ppermute | solution.py:455
  86.5 0.6 copy-done.9
  87.2 7.2 %step_two.1 = (f32[2,16,32]{2,1,0:T(8,128)}, f32[8,512,128]{2,1,0:T(8,128)}) custom-call(f32[8,512,128]{2,1,0:T(8,128)} %get-tuple-element.28.density.fields, f32[16,128]{1,0:T(8,128)} %get-tuple-element.29.own, f32[400,128]{1,0:T(8,128)} %copy-done, f32[400,128]{1,0:T(8,128)} %copy-done.1, f32[120,128]{1,0:T(8,128)} %copy-done.8, f32[120,128]{1,0:T(8,128)} %copy-done.9, ...), custom_call_target="tpu_custom_call" | custom-call | tf_op jit(solution)/shard_map/step_two/pallas_call | solution.py:518
  (21 shorter events, 0.1 us)
Async XLA Ops:
  2.7 9.7 %collective-permute-start = (f32[144,128]{1,0:T(8,128)}, f32[144,128]{1,0:T(8,128)S(1)}, u32[]{:S(2)}, u32[]{:S(2)}) collective-permute-start(f32[144,128]{1,0:T(8,128)} %get-tuple-element.20), channel_id=1, source_target_pairs={{0,16},{16,0},{32,48},{48,32},{64,80},{80,64},{96,112},{112,96},{1... | collective-permute-start | bytes 221192 | tf_op jit(solution)/shard_map/ppermute | solution.py:455
  4.6 14.3 %collective-permute-start.1 = (f32[144,128]{1,0:T(8,128)}, f32[144,128]{1,0:T(8,128)S(1)}, u32[]{:S(2)}, u32[]{:S(2)}) collective-permute-start(f32[144,128]{1,0:T(8,128)} %get-tuple-element.21), channel_id=1, source_target_pairs={{16,32},{32,16},{48,64},{64,48},{80,96},{96,80},{112,128},{128,112... | collective-permute-start | bytes 221192 | tf_op jit(solution)/shard_map/ppermute | solution.py:455
  12.4 6.5 %copy-start.2 = (f32[144,128]{1,0:T(8,128)}, f32[144,128]{1,0:T(8,128)S(1)}, u32[]{:S(2)}) copy-start(f32[144,128]{1,0:T(8,128)S(1)} %collective-permute-done.halo_even) | copy-start | bytes 221188
  18.9 0.6 copy-start.3
  22.9 20.3 %collective-permute-start.4 = (f32[264,128]{1,0:T(8,128)}, f32[264,128]{1,0:T(8,128)S(1)}, u32[]{:S(2)}, u32[]{:S(2)}) collective-permute-start(f32[264,128]{1,0:T(8,128)} %get-tuple-element.24), channel_id=1, source_target_pairs={{0,16},{16,0},{32,48},{48,32},{64,80},{80,64},{96,112},{112,96},{1... | collective-permute-start | bytes 405512 | tf_op jit(solution)/shard_map/ppermute | solution.py:455
  24.8 18.3 %collective-permute-start.5 = (f32[264,128]{1,0:T(8,128)}, f32[264,128]{1,0:T(8,128)S(1)}, u32[]{:S(2)}, u32[]{:S(2)}) collective-permute-start(f32[264,128]{1,0:T(8,128)} %get-tuple-element.25), channel_id=1, source_target_pairs={{16,32},{32,16},{48,64},{64,48},{80,96},{96,80},{112,128},{128,112... | collective-permute-start | bytes 405512 | tf_op jit(solution)/shard_map/ppermute | solution.py:455
  30.5 9.1 %collective-permute-start.2 = (f32[120,128]{1,0:T(8,128)}, f32[120,128]{1,0:T(8,128)S(1)}, u32[]{:S(2)}, u32[]{:S(2)}) collective-permute-start(f32[120,128]{1,0:T(8,128)} %get-tuple-element.22), channel_id=1, source_target_pairs={{0,1},{1,0},{2,3},{3,2},{4,5},{5,4},{6,7},{7,6},{8,9},{9,8},{10,11... | collective-permute-start | bytes 184328 | tf_op jit(solution)/shard_map/ppermute | solution.py:455
  34.1 9.0 %collective-permute-start.3 = (f32[120,128]{1,0:T(8,128)}, f32[120,128]{1,0:T(8,128)S(1)}, u32[]{:S(2)}, u32[]{:S(2)}) collective-permute-start(f32[120,128]{1,0:T(8,128)} %get-tuple-element.23), channel_id=1, source_target_pairs={{1,2},{2,1},{3,4},{4,3},{5,6},{6,5},{7,8},{8,7},{9,10},{10,9},{11,... | collective-permute-start | bytes 184328 | tf_op jit(solution)/shard_map/ppermute | solution.py:455
  39.6 3.5 %copy-start.6 = (f32[120,128]{1,0:T(8,128)}, f32[120,128]{1,0:T(8,128)S(1)}, u32[]{:S(2)}) copy-start(f32[120,128]{1,0:T(8,128)S(1)} %collective-permute-done.2.y_even) | copy-start | bytes 184324
  43.1 0.6 copy-start.7
  43.1 0.7 copy-start.4
  43.1 0.7 copy-start.5
  51.6 5.1 %collective-permute-start.6 = (f32[400,128]{1,0:T(8,128)}, f32[400,128]{1,0:T(8,128)S(1)}, u32[]{:S(2)}, u32[]{:S(2)}) collective-permute-start(f32[400,128]{1,0:T(8,128)} %get-tuple-element.30), channel_id=1, source_target_pairs={{0,16},{16,0},{32,48},{48,32},{64,80},{80,64},{96,112},{112,96},{1... | collective-permute-start | bytes 614408 | tf_op jit(solution)/shard_map/ppermute | solution.py:455
  53.5 14.1 %collective-permute-start.7 = (f32[400,128]{1,0:T(8,128)}, f32[400,128]{1,0:T(8,128)S(1)}, u32[]{:S(2)}, u32[]{:S(2)}) collective-permute-start(f32[400,128]{1,0:T(8,128)} %get-tuple-element.31), channel_id=1, source_target_pairs={{16,32},{32,16},{48,64},{64,48},{80,96},{96,80},{112,128},{128,112... | collective-permute-start | bytes 614408 | tf_op jit(solution)/shard_map/ppermute | solution.py:455
  56.7 10.9 %copy-start = (f32[400,128]{1,0:T(8,128)}, f32[400,128]{1,0:T(8,128)S(1)}, u32[]{:S(2)}) copy-start(f32[400,128]{1,0:T(8,128)S(1)} %collective-permute-done.6.halo_even.x_even) | copy-start | bytes 614404
  67.6 0.7 copy-start.1
  70.1 11.1 %collective-permute-start.8 = (f32[120,128]{1,0:T(8,128)}, f32[120,128]{1,0:T(8,128)S(1)}, u32[]{:S(2)}, u32[]{:S(2)}) collective-permute-start(f32[120,128]{1,0:T(8,128)} %get-tuple-element.32), channel_id=1, source_target_pairs={{0,1},{1,0},{2,3},{3,2},{4,5},{5,4},{6,7},{7,6},{8,9},{9,8},{10,11... | collective-permute-start | bytes 184328 | tf_op jit(solution)/shard_map/ppermute | solution.py:455
  77.5 9.0 %collective-permute-start.9 = (f32[120,128]{1,0:T(8,128)}, f32[120,128]{1,0:T(8,128)S(1)}, u32[]{:S(2)}, u32[]{:S(2)}) collective-permute-start(f32[120,128]{1,0:T(8,128)} %get-tuple-element.33), channel_id=1, source_target_pairs={{1,2},{2,1},{3,4},{4,3},{5,6},{6,5},{7,8},{8,7},{9,10},{10,9},{11,... | collective-permute-start | bytes 184328 | tf_op jit(solution)/shard_map/ppermute | solution.py:455
  81.2 5.3 %copy-start.8 = (f32[120,128]{1,0:T(8,128)}, f32[120,128]{1,0:T(8,128)S(1)}, u32[]{:S(2)}) copy-start(f32[120,128]{1,0:T(8,128)S(1)} %collective-permute-done.8.y_even) | copy-start | bytes 184324
  86.5 0.6 copy-start.9

commit v2 on v1

--- a/solution.py
+++ b/solution.py
@@ -33,13 +33,12 @@
 DONOR_ROWS = FIELDS * CAP
 REQUEST_MSG = AT_REST + 8
 DONOR_MSG = DONOR_ROWS + 8
-FULL_MSG = AT_REST + DONOR_MSG
 Y_DENSITY = EXT * HALO
 Y_MSG = Y_DENSITY + EXT
 
 F32 = jnp.float32
 BF16 = jnp.bfloat16
-VMEM_BYTES = 56 * 1024 * 1024
+VMEM_BYTES = 20 * 1024 * 1024
 
 
 def iota(shape, dim):
@@ -65,8 +64,26 @@
     return tile_x, tile_y, lax.rem(tile_x, 2), lax.rem(tile_y, 2)
 
 
-def first_kernel(disp, head, tail, owner, place, out_even, out_odd, own, aux):
+def first_kernel(
+    disp_hbm, fields_hbm, owner_hbm, place_hbm, out_even, out_odd, own, aux, disp, head, tail, owner, place, sems
+):
     tile_x, _, px, _ = parities()
+    copies = [
+        pltpu.make_async_copy(source, target, sems.at[i])
+        for i, (source, target) in enumerate(
+            (
+                (owner_hbm, owner),
+                (place_hbm, place),
+                (disp_hbm, disp),
+                (fields_hbm.at[0, pl.ds(0, EDGE)], head),
+                (fields_hbm.at[0, pl.ds(TILE - EDGE, EDGE)], tail),
+            )
+        )
+    ]
+    for copy in copies:
+        copy.start()
+    for copy in copies:
+        copy.wait()
     offsets = spread(disp[0], disp[1])
     own[...] = offsets
     first_owner = owner[:, 0, :]
@@ -94,7 +111,7 @@
         )
     request = jnp.broadcast_to(jnp.sum(asked, axis=0, keepdims=True), (8, LANES))
     aux[CX:, :] = request
-    low, high = head[0], tail[0]
+    low, high = head[...], tail[...]
     out_even[:EDGE, :] = pick(px, low, high)
     out_odd[:EDGE, :] = pick(px, high, low)
     low, high = offsets[:8], offsets[8:]
@@ -137,12 +154,12 @@
     out_odd[Y_DENSITY:, :] = ext[...]
 
 
-def take_donors(fields, places, out_even, out_odd, start):
+def take_donors(fields, places, out_even, out_odd):
     def one(r, carry):
         for out, shift in ((out_even, 0), (out_odd, CAP)):
             p = places[0, r + shift]
             for f in range(FIELDS):
-                out[pl.ds(start + f * CAP + r, 1), :] = fields[f, pl.ds(p, 1), :]
+                out[pl.ds(f * CAP + r, 1), :] = fields[f, pl.ds(p, 1), :]
         return carry
 
     lax.fori_loop(0, CAP, one, 0, unroll=8)
@@ -164,7 +181,7 @@
     return outs
 
 
-def donor_offsets(own, asked, out_even, out_odd, start):
+def donor_offsets(own, asked, out_even, out_odd):
     flat_x, flat_y = flat_rows(own)
     sub = iota((HALF, LANES), 0)
     lane = iota((HALF, LANES), 1)
@@ -178,14 +195,12 @@
         rows.append(jnp.sum(jnp.where(sub == lane, column, 0.0), axis=0, keepdims=True))
     place = iota((8, LANES), 0)
     even = jnp.where(place == 0, rows[0], jnp.where(place == 1, rows[1], 0.0))
-    out_even[start : start + 8, :] = even
-    out_odd[start : start + 8, :] = pltpu.roll(even, LANES - CAP, 1)
-
-
-def second_kernel(
-    fields, own, halo_even, halo_odd, y_even, y_odd, donor_even, donor_odd, asked_out, ext, places, sem
-):
-    _, _, px, py = parities()
+    out_even[DONOR_ROWS:, :] = even
+    out_odd[DONOR_ROWS:, :] = pltpu.roll(even, LANES - CAP, 1)
+
+
+def donor_kernel(fields, own, halo_odd, halo_even, after, donor_even, donor_odd, asked_out, places, sem):
+    _, _, px, _ = parities()
     lane = iota((8, LANES), 1)
     even = halo_even[AT_REST:, :]
     odd = halo_odd[AT_REST:, :]
@@ -197,13 +212,12 @@
     asked_out[...] = asked.astype(jnp.int32)
     copy = pltpu.make_async_copy(asked_out, places, sem)
     copy.start()
-    pack_y(fields[0], halo_even, halo_odd, own[...], ext, px, py, y_even, y_odd)
-    donor_offsets(own[...], asked[:1], donor_even, donor_odd, DONOR_ROWS)
+    donor_offsets(own[...], asked[:1], donor_even, donor_odd)
     copy.wait()
-    take_donors(fields, places, donor_even, donor_odd, 0)
-
-
-def third_kernel(density, own, halo_even, halo_odd, y_even, y_odd, ext):
+    take_donors(fields, places, donor_even, donor_odd)
+
+
+def columns_kernel(density, own, halo_odd, halo_even, y_even, y_odd, ext):
     _, _, px, py = parities()
     pack_y(density[0], halo_even, halo_odd, own[...], ext, px, py, y_even, y_odd)
 
@@ -288,16 +302,57 @@
     return ext[HALO : HALO + CX, :]
 
 
-def weigh(own, moved, owner, place, count, aux, offsets_even, offsets_odd, left_hand, inverse):
-    tile_x, _, px, _ = parities()
+def weight(dx, dy):
+    bulk = SPREAD_SQ + dx * dx + dy * dy
+    guess = pl.reciprocal(bulk, approx=True)
+    return guess * (2.0 - bulk * guess)
+
+
+def split(x):
+    high = x.astype(BF16)
+    return high, (x - high.astype(F32)).astype(BF16)
+
+
+def placed(shifts, r):
+    along = iota((CY, 1), 0).astype(F32)
+    at_x = shifts[SIDE : SIDE + CY, r : r + 1] + float(r)
+    at_y = shifts[HALF + SIDE : HALF + SIDE + CY, r : r + 1] + along
+    return at_x, at_y
+
+
+def weigh_near(own, moved, owner, place, count, left_hand, norm):
+    tile_x = lax.axis_index("gx")
     flat_x, flat_y = flat_rows(own)
     spot = iota((1, TILE), 1)
     flat_x = flat_x + (spot // CY).astype(F32)
     flat_y = flat_y + lax.rem(spot, CY).astype(F32)
-
+    live = count[...]
+    codes = []
+    for k in range(DONORS):
+        here = owner[:, k, :] == tile_x
+        codes.append(widen(jnp.where(here & (k < live), place[:, k, :], -1).astype(F32)))
+    columns = jnp.transpose(jnp.concatenate(codes, axis=0))
+    shifts = jnp.transpose(moved)
+    spots = iota((CY, TILE), 1).astype(F32)
+    for r in range(CX):
+        at_x, at_y = placed(shifts, r)
+        dense = weight(at_x - flat_x, at_y - flat_y)
+        total = jnp.zeros((CY, TILE), F32)
+        for k in range(DONORS):
+            code = columns[:CY, k * CX + r : k * CX + r + 1]
+            total = total + jnp.where(code == spots, dense, 0.0)
+        rows = slice(r * CY, (r + 1) * CY)
+        norm[rows, :] = jnp.broadcast_to(jnp.sum(total, axis=1, keepdims=True), (CY, LANES))
+        high, low = split(total)
+        left_hand[rows, 0:TILE] = high
+        left_hand[rows, TILE : 2 * TILE] = low
+        left_hand[rows, 2 * TILE : 3 * TILE] = high
+
+
+def weigh_far(moved, aux, even, odd, norm, left_hand, inverse):
+    _, _, px, _ = parities()
     request = aux[CX : CX + 1, :].astype(jnp.int32)
     lane = iota((1, LANES), 1)
-    even, odd = offsets_even, offsets_odd
     left = pick(px, even, odd)
     right = pick(px, odd, even)
     far = jnp.where(iota((8, LANES), 1) < CAP, left, pltpu.roll(right, CAP, 1))
@@ -307,142 +362,120 @@
     far_y = jnp.where(lane < HALF, far_y, pltpu.roll(far_y, HALF, 1))
     far_lane = lax.rem(lane, HALF).astype(F32)
     near_half = iota((CY, LANES), 1) < HALF
-
-    live = count[...]
-    codes = []
-    for k in range(DONORS):
-        here = owner[:, k, :] == tile_x
-        codes.append(widen(jnp.where(here & (k < live), place[:, k, :], -1).astype(F32)))
-    codes.append(jnp.where(widen(live.astype(F32)) > 0, aux[:CX, :], -1.0))
-    columns = jnp.transpose(jnp.concatenate(codes, axis=0))
+    columns = jnp.transpose(aux[...])
     shifts = jnp.transpose(moved)
-    along = iota((CY, 1), 0).astype(F32)
-    spots = iota((CY, TILE), 1).astype(F32)
-
-    def weight(dx, dy):
-        bulk = SPREAD_SQ + dx * dx + dy * dy
-        guess = pl.reciprocal(bulk, approx=True)
-        return guess * (2.0 - bulk * guess)
-
     for r in range(CX):
-        at_x = shifts[SIDE : SIDE + CY, r : r + 1] + float(r)
-        at_y = shifts[HALF + SIDE : HALF + SIDE + CY, r : r + 1] + along
-        dense = weight(at_x - flat_x, at_y - flat_y)
-        total = jnp.zeros((CY, TILE), F32)
-        for k in range(DONORS):
-            code = columns[:CY, k * CX + r : k * CX + r + 1]
-            total = total + jnp.where(code == spots, dense, 0.0)
-        code = columns[:CY, DONORS * CX + r : DONORS * CX + r + 1]
+        at_x, at_y = placed(shifts, r)
+        code = columns[:CY, r : r + 1]
         remote = jnp.where(code == far_lane, weight(at_x - far_x, at_y - far_y), 0.0)
-        norm = jnp.sum(total, axis=1, keepdims=True) + jnp.sum(
-            jnp.where(near_half, remote, 0.0), axis=1, keepdims=True
-        )
         rows = slice(r * CY, (r + 1) * CY)
-        inverse[rows, :] = jnp.broadcast_to(1.0 / norm, (CY, LANES))
-        high = total.astype(BF16)
-        left_hand[rows, 0:TILE] = high
-        left_hand[rows, TILE : 2 * TILE] = (total - high.astype(F32)).astype(BF16)
-        left_hand[rows, 2 * TILE : 3 * TILE] = high
-        high = remote.astype(BF16)
-        low = (remote - high.astype(F32)).astype(BF16)
-        base = 3 * TILE
-        left_hand[rows, base : base + LANES] = jnp.where(near_half, high.astype(F32), low.astype(F32)).astype(BF16)
-        left_hand[rows, base + LANES : base + 2 * LANES] = jnp.where(near_half, high.astype(F32), 0.0).astype(BF16)
-
-
-def split(x):
-    high = x.astype(BF16)
-    return high, (x - high.astype(F32)).astype(BF16)
-
-
-def combine(fields, donors_even, donors_odd, px, left_hand, right_hand, inverse, out):
+        total = norm[rows, :] + jnp.sum(jnp.where(near_half, remote, 0.0), axis=1, keepdims=True)
+        inverse[rows, :] = 1.0 / total
+        high = remote.astype(BF16).astype(F32)
+        left_hand[rows, :LANES] = jnp.where(near_half, high, remote - high).astype(BF16)
+        left_hand[rows, LANES:] = jnp.where(near_half, high, 0.0).astype(BF16)
+
+
+def mix_near(fields, left_hand, right_hand, out):
     for f in range(FIELDS):
         n, lanes = f // 2, slice((f % 2) * NZ, (f % 2) * NZ + NZ)
         high, low = split(fields[f])
         right_hand[n, 0:TILE, lanes] = high
         right_hand[n, TILE : 2 * TILE, lanes] = high
         right_hand[n, 2 * TILE : 3 * TILE, lanes] = low
-        even = donors_even(f)
-        odd = donors_odd(f)
-        both = jnp.concatenate([pick(px, even, odd), pick(px, odd, even)], axis=0)
-        high, low = split(both)
-        base = 3 * TILE
-        right_hand[n, base : base + HALF, lanes] = high
-        right_hand[n, base + HALF : base + 2 * HALF, lanes] = high
-        right_hand[n, base + 2 * HALF : base + 3 * HALF, lanes] = low
-        right_hand[n, base + 3 * HALF : base + 4 * HALF, lanes] = jnp.zeros((HALF, NZ), BF16)
-
     for n in range(FIELDS // 2):
         mixed = jnp.dot(left_hand[...], right_hand[n], preferred_element_type=F32)
-        out[2 * n] = mixed[:, :NZ] * inverse[...]
-        out[2 * n + 1] = mixed[:, NZ:] * inverse[...]
-
-
-def step_kernel(
-    fields, own, halo_even, halo_odd, y_even, y_odd, donor_even, donor_odd, owner, place, count, aux, asked,
-    out, own_out, x_even, x_odd,
-    dens, ext, mon, left_hand, right_hand, inverse, places, sem,
+        out[2 * n] = mixed[:, :NZ]
+        out[2 * n + 1] = mixed[:, NZ:]
+
+
+def mix_far(near, even, odd, left_hand, right_hand, inverse, out, done=None):
+    _, _, px, _ = parities()
+    for f in range(FIELDS):
+        n, lanes = f // 2, slice((f % 2) * NZ, (f % 2) * NZ + NZ)
+        from_even = even[f * CAP : (f + 1) * CAP, :]
+        from_odd = odd[f * CAP : (f + 1) * CAP, :]
+        left, right = pick(px, from_even, from_odd), pick(px, from_odd, from_even)
+        high, low = split(jnp.concatenate([left, right], axis=0))
+        right_hand[n, 0:HALF, lanes] = high
+        right_hand[n, HALF : 2 * HALF, lanes] = high
+        right_hand[n, 2 * HALF : 3 * HALF, lanes] = low
+        right_hand[n, 3 * HALF :, lanes] = jnp.zeros((HALF, NZ), BF16)
+    for n in range(FIELDS // 2):
+        mixed = jnp.dot(left_hand[...], right_hand[n], preferred_element_type=F32)
+        out[2 * n] = (near[2 * n] + mixed[:, :NZ]) * inverse[...]
+        out[2 * n + 1] = (near[2 * n + 1] + mixed[:, NZ:]) * inverse[...]
+        if done is not None:
+            done(n)
+
+
+def near_kernel(
+    fields, own, halo_odd, halo_even, y_odd, y_even, owner, place, count,
+    near, moved_out, norm,
+    dens, ext, mon, left_hand, right_hand,
+):
+    moved = relax(fields, own[...], halo_even, halo_odd, y_even, y_odd, dens, ext, mon)
+    moved_out[...] = moved
+    weigh_near(own[...], moved, owner, place, count, left_hand, norm)
+    mix_near(fields, left_hand, right_hand, near)
+
+
+def far_kernel(
+    near, moved, norm, donor_odd, donor_even, aux, asked,
+    out, x_even, x_odd, d_even, d_odd,
+    left_hand, right_hand, inverse, places, sem,
 ):
     _, _, px, _ = parities()
     copy = pltpu.make_async_copy(asked, places, sem)
     copy.start()
-    moved = relax(fields, own[...], halo_even, halo_odd, y_even, y_odd, dens, ext, mon)
-    own_out[...] = moved
-    weigh(
-        own[...], moved, owner, place, count, aux,
-        donor_even[DONOR_ROWS:, :], donor_odd[DONOR_ROWS:, :], left_hand, inverse,
-    )
-    combine(
-        fields,
-        lambda f: donor_even[f * CAP : (f + 1) * CAP, :],
-        lambda f: donor_odd[f * CAP : (f + 1) * CAP, :],
-        px, left_hand, right_hand, inverse, out,
-    )
+    weigh_far(
+        moved[...], aux, donor_even[DONOR_ROWS:, :], donor_odd[DONOR_ROWS:, :], norm, left_hand, inverse
+    )
+    mix_far(near, donor_even, donor_odd, left_hand, right_hand, inverse, out)
     low, high = out[0, :EDGE, :], out[0, TILE - EDGE :, :]
     x_even[:EDGE, :] = pick(px, low, high)
     x_odd[:EDGE, :] = pick(px, high, low)
-    low, high = moved[:8], moved[8:]
+    low, high = moved[:8, :], moved[8:, :]
     x_even[AT_OFFSETS:AT_REST, :] = pick(px, low, high)
     x_odd[AT_OFFSETS:AT_REST, :] = pick(px, high, low)
-    donor_offsets(moved, asked[:1, :].astype(F32), x_even, x_odd, AT_REST + DONOR_ROWS)
+    donor_offsets(moved[...], asked[:1, :].astype(F32), d_even, d_odd)
     copy.wait()
-    take_donors(out, places, x_even, x_odd, AT_REST)
+    take_donors(out, places, d_even, d_odd)
 
 
 def last_kernel(
-    fields, own, x_even, x_odd, y_even, y_odd, owner, place, count, aux,
-    moved_out, out,
-    dens, ext, mon, left_hand, right_hand, inverse,
+    near, moved, norm, donor_odd, donor_even, aux,
+    moved_out, out_hbm,
+    left_hand, right_hand, inverse, out, sems,
 ):
-    _, _, px, _ = parities()
-    moved = relax(fields, own[...], x_even, x_odd, y_even, y_odd, dens, ext, mon)
-    moved_out[0] = pltpu.roll(moved, LANES - SIDE, 1)[:, :CY]
-    moved_out[1] = pltpu.roll(moved, HALF - SIDE, 1)[:, :CY]
-    at = AT_REST + DONOR_ROWS
-    weigh(
-        own[...], moved, owner, place, count, aux,
-        x_even[at : at + 8, :], x_odd[at : at + 8, :], left_hand, inverse,
-    )
-    combine(
-        fields,
-        lambda f: x_even[AT_REST + f * CAP : AT_REST + (f + 1) * CAP, :],
-        lambda f: x_odd[AT_REST + f * CAP : AT_REST + (f + 1) * CAP, :],
-        px, left_hand, right_hand, inverse, out,
-    )
+    wide = moved[...]
+    moved_out[0] = pltpu.roll(wide, LANES - SIDE, 1)[:, :CY]
+    moved_out[1] = pltpu.roll(wide, HALF - SIDE, 1)[:, :CY]
+    weigh_far(wide, aux, donor_even[DONOR_ROWS:, :], donor_odd[DONOR_ROWS:, :], norm, left_hand, inverse)
+
+    def copy(n):
+        pair = pl.ds(2 * n, 2)
+        return pltpu.make_async_copy(out.at[pair], out_hbm.at[pair], sems.at[n])
+
+    mix_far(
+        near, donor_even, donor_odd, left_hand, right_hand, inverse, out, lambda n: copy(n).start()
+    )
+    for n in range(FIELDS // 2):
+        copy(n).wait()
 
 
 def shape(*dims, dtype=F32):
     return jax.ShapeDtypeStruct(dims, dtype)
 
 
-def call(kernel, outs, scratch=(), in_specs=None, name=None):
-    extra = {} if in_specs is None else {"in_specs": in_specs, "grid": (1,)}
+def call(kernel, outs, scratch=(), name=None, cost=None, **extra):
     return pl.pallas_call(
         kernel,
         out_shape=outs,
         scratch_shapes=list(scratch),
         compiler_params=pltpu.CompilerParams(vmem_limit_bytes=VMEM_BYTES),
         name=name,
+        cost_estimate=cost,
         **extra,
     )
 
@@ -456,16 +489,24 @@
 
 
 def swap(even, odd, axis):
-    return swap_pairs(even, axis, False), swap_pairs(odd, axis, True)
-
-
-WORK = (
+    odd = swap_pairs(odd, axis, True)
+    return swap_pairs(even, axis, False), odd
+
+
+RELAX = (
     pltpu.VMEM((EXT, WIDE, NZ), F32),
     pltpu.VMEM((EXT, LANES), F32),
     pltpu.VMEM((EXT, LANES), F32),
-    pltpu.VMEM((TILE, 3 * TILE + 4 * HALF), BF16),
-    pltpu.VMEM((FIELDS // 2, 3 * TILE + 4 * HALF, 2 * NZ), BF16),
-    pltpu.VMEM((TILE, LANES), F32),
+)
+NEAR = (
+    pltpu.VMEM((TILE, 3 * TILE), BF16),
+    pltpu.VMEM((FIELDS // 2, 3 * TILE, 2 * NZ), BF16),
+)
+NORM = pltpu.VMEM((TILE, LANES), F32)
+FAR = (
+    pltpu.VMEM((TILE, 4 * HALF), BF16),
+    pltpu.VMEM((FIELDS // 2, 4 * HALF, 2 * NZ), BF16),
+    NORM,
 )
 PLACES = (pltpu.SMEM((8, LANES), jnp.int32), pltpu.SemaphoreType.DMA)
 
@@ -474,8 +515,27 @@
     return pl.BlockSpec(memory_space=pltpu.VMEM)
 
 
-def density_rows(start, rows):
-    return pl.BlockSpec((1, rows, NZ), lambda i: (0, start // rows, 0))
+def columns(fields, own, halo):
+    return call(
+        columns_kernel,
+        (shape(Y_MSG, LANES), shape(Y_MSG, LANES)),
+        scratch=(pltpu.VMEM((EXT, LANES), F32),),
+        grid=(1,),
+        in_specs=[pl.BlockSpec((1, TILE, NZ), lambda i: (0, 0, 0)), whole(), whole(), whole()],
+        name="pack_columns",
+    )(fields, own, *halo[::-1])
+
+
+def step_near(fields, own, halo, y_halo, owner, place, count):
+    return call(
+        near_kernel,
+        (shape(FIELDS, TILE, NZ), shape(CX, LANES), shape(TILE, LANES)),
+        scratch=RELAX + NEAR,
+        name="step_near",
+        cost=pl.CostEstimate(
+            flops=2 * TILE * 3 * TILE * FIELDS * NZ, bytes_accessed=16 << 20, transcendentals=TILE * TILE
+        ),
+    )(fields, own, *halo[::-1], *y_halo[::-1], owner, place, count)
 
 
 def per_device(fields, displacement, donor_tile, donor_offset, donor_count):
@@ -485,42 +545,48 @@
     even, odd, own, aux = call(
         first_kernel,
         (shape(REQUEST_MSG, LANES), shape(REQUEST_MSG, LANES), shape(CX, LANES), shape(CX + 8, LANES)),
-        in_specs=[whole(), density_rows(0, EDGE), density_rows(TILE - EDGE, EDGE), whole(), whole()],
+        scratch=(
+            pltpu.VMEM((2, CX, CY), F32),
+            pltpu.VMEM((EDGE, NZ), F32),
+            pltpu.VMEM((EDGE, NZ), F32),
+            pltpu.VMEM((CX, DONORS, CY), jnp.int32),
+            pltpu.VMEM((CX, DONORS, CY), jnp.int32),
+            pltpu.SemaphoreType.DMA((5,)),
+        ),
+        in_specs=[pl.BlockSpec(memory_space=pltpu.HBM)] * 4,
         name="pack_first",
-    )(displacement, fields, fields, owner, place)
+    )(*(pltpu.with_memory_space_constraint(x, pltpu.HBM) for x in (displacement, fields, owner, place)))
     halo = swap(even, odd, "gx")
-    y_even, y_odd, d_even, d_odd, asked = call(
-        second_kernel,
+    y_even, y_odd = columns(fields, own, halo)
+    y_halo = swap(y_even, y_odd, "gy")
+    d_even, d_odd, asked = call(
+        donor_kernel,
+        (shape(DONOR_MSG, LANES), shape(DONOR_MSG, LANES), shape(8, LANES, dtype=jnp.int32)),
+        scratch=PLACES,
+        name="pack_donors",
+    )(fields, own, *halo[::-1], y_even)
+    donors = swap(d_even, d_odd, "gx")
+    near, own, norm = step_near(fields, own, halo, y_halo, owner, place, donor_count)
+    fields, even, odd, d_even, d_odd = call(
+        far_kernel,
         (
-            shape(Y_MSG, LANES), shape(Y_MSG, LANES), shape(DONOR_MSG, LANES), shape(DONOR_MSG, LANES),
-            shape(8, LANES, dtype=jnp.int32),
+            shape(FIELDS, TILE, NZ), shape(AT_REST, LANES), shape(AT_REST, LANES),
+            shape(DONOR_MSG, LANES), shape(DONOR_MSG, LANES),
         ),
-        scratch=(pltpu.VMEM((EXT, LANES), F32),) + PLACES,
-        name="pack_donors",
-    )(fields, own, *halo)
-    y_halo = swap(y_even, y_odd, "gy")
+        scratch=FAR + PLACES,
+        name="step_one_far",
+    )(near, own, norm, *donors[::-1], aux, asked)
+    halo = swap(even, odd, "gx")
+    y_halo = swap(*columns(fields, own, halo), "gy")
     donors = swap(d_even, d_odd, "gx")
-    fields, own, even, odd = call(
-        step_kernel,
-        (shape(FIELDS, TILE, NZ), shape(CX, LANES), shape(FULL_MSG, LANES), shape(FULL_MSG, LANES)),
-        scratch=WORK + PLACES,
-        name="step_one",
-    )(fields, own, *halo, *y_halo, *donors, owner, place, donor_count, aux, asked)
-    halo = swap(even, odd, "gx")
-    y_even, y_odd = call(
-        third_kernel,
-        (shape(Y_MSG, LANES), shape(Y_MSG, LANES)),
-        scratch=(pltpu.VMEM((EXT, LANES), F32),),
-        in_specs=[density_rows(0, TILE), whole(), whole(), whole()],
-        name="pack_y",
-    )(fields, own, *halo)
-    y_halo = swap(y_even, y_odd, "gy")
+    near, own, norm = step_near(fields, own, halo, y_halo, owner, place, donor_count)
     moved, fields = call(
         last_kernel,
         (shape(2, CX, CY), shape(FIELDS, TILE, NZ)),
-        scratch=WORK,
-        name="step_two",
-    )(fields, own, *halo, *y_halo, owner, place, donor_count, aux)
+        scratch=FAR + (pltpu.VMEM((FIELDS, TILE, NZ), F32), pltpu.SemaphoreType.DMA((FIELDS // 2,))),
+        out_specs=(whole(), pl.BlockSpec(memory_space=pltpu.HBM)),
+        name="step_two_far",
+    )(near, own, norm, *donors[::-1], aux)
     return moved, fields.reshape(FIELDS, CX, CY, NZ)
 
 

time: 94.9 us -> 79.8 us (0.84)
  the two profiles are of different devices: /device:TPU:480 before, /device:TPU:424 now
where the time goes in v2:
time: 79.8 us; the launch traced here: 79.4 us
  starting transfers between devices  43 us (54%)
  waiting for transfers between devices  20.3 us (25%)
  Pallas kernels  15.2 us (19%)
  between operations  0.85 us (1%)
    ppermute x12, starting transfers between devices, swap_pairs(): return lax.ppermute(block, axis, route)  43 us
    ppermute x12, waiting for transfers between devices, swap_pairs(): return lax.ppermute(block, axis, route)  20.3 us
    pallas_call x2, Pallas kernels, step_near(): call(near_kernel, (shape(FIELDS, TILE, NZ), shape(CX, LANES), shape(TILE,...  7.16 us
    pallas_call x1, Pallas kernels, per_device(): call(last_kernel, (shape(2, CX, CY), shape(FIELDS, TILE, NZ)), scratch=FA...  3.27 us
    pallas_call x1, Pallas kernels, per_device(): call(far_kernel, (shape(FIELDS, TILE, NZ), shape(AT_REST, LANES), shape(A...  2.13 us
    pallas_call x1, Pallas kernels, per_device(): call(first_kernel, (shape(REQUEST_MSG, LANES), shape(REQUEST_MSG, LANES),...  1.62 us
  transfers between devices with their start and end apart: 12, of which 4 were waited for; matrix products, arithmetic and copies ran while one was open for 0% of the time, Pallas kernels for 10%

profile of v2, /device:TPU:424, one launch (start us, length us, event | category | flops | bytes accessed | tf_op | source)
XLA Modules:
  0.0 79.4 jit_solution(6916356684366767043)
XLA Ops:
  0.6 1.6 %pack_first.1 = (f32[144,128]{1,0:T(8,128)S(1)}, f32[144,128]{1,0:T(8,128)S(1)}, f32[16,128]{1,0:T(8,128)S(1)}, f32[24,128]{1,0:T(8,128)S(1)}) custom-call(f32[2,16,32]{2,1,0:T(8,128)} %disp_hbm.1, f32[8,512,128]{2,1,0:T(8,128)} %bitcast.4, s32[16,4,32]{2,1,0:T(4,128)} %bitcast.8, s32[16,4,32]{2,1,0:T(4,128)} %bitcast.11), custom_call_target="tpu_custom_call" | custom-call | tf_op jit(solution)/shard_map/pack_first/pallas_call | solution.py:545
  2.3 7.1 %collective-permute-start = (f32[144,128]{1,0:T(8,128)S(1)}, f32[144,128]{1,0:T(8,128)S(1)}, u32[]{:S(2)}, u32[]{:S(2)}) collective-permute-start(f32[144,128]{1,0:T(8,128)S(1)} %get-tuple-element.27), channel_id=1, source_target_pairs={{16,32},{32,16},{48,64},{64,48},{80,96},{96,80},{112,128},{128,112... | collective-permute-start | bytes 221192 | tf_op jit(solution)/shard_map/ppermute | solution.py:488
  9.4 1.9 %collective-permute-start.1 = (f32[144,128]{1,0:T(8,128)S(1)}, f32[144,128]{1,0:T(8,128)S(1)}, u32[]{:S(2)}, u32[]{:S(2)}) collective-permute-start(f32[144,128]{1,0:T(8,128)S(1)} %get-tuple-element.28), channel_id=1, source_target_pairs={{0,16},{16,0},{32,48},{48,32},{64,80},{80,64},{96,112},{112,96},{1... | collective-permute-start | bytes 221192 | tf_op jit(solution)/shard_map/ppermute | solution.py:488
  11.3 3.6 %collective-permute-done.halo_odd = f32[144,128]{1,0:T(8,128)S(1)} collective-permute-done((f32[144,128]{1,0:T(8,128)S(1)}, f32[144,128]{1,0:T(8,128)S(1)}, u32[]{:S(2)}, u32[]{:S(2)}) %collective-permute-start) | collective-permute-done | bytes 73760 | tf_op jit(solution)/shard_map/ppermute | solution.py:488
  15.0 0.0 copy-start.2
  15.0 0.0 copy-start.3
  15.0 3.6 %collective-permute-start.2 = (f32[120,128]{1,0:T(8,128)S(1)}, f32[120,128]{1,0:T(8,128)S(1)}, u32[]{:S(2)}, u32[]{:S(2)}) collective-permute-start(f32[120,128]{1,0:T(8,128)S(1)} %get-tuple-element.29), channel_id=1, source_target_pairs={{1,2},{2,1},{3,4},{4,3},{5,6},{6,5},{7,8},{8,7},{9,10},{10,9},{11,... | collective-permute-start | bytes 184328 | tf_op jit(solution)/shard_map/ppermute | solution.py:488
  18.6 4.4 %collective-permute-start.3 = (f32[120,128]{1,0:T(8,128)S(1)}, f32[120,128]{1,0:T(8,128)S(1)}, u32[]{:S(2)}, u32[]{:S(2)}) collective-permute-start(f32[120,128]{1,0:T(8,128)S(1)} %get-tuple-element.30.after), channel_id=1, source_target_pairs={{0,1},{1,0},{2,3},{3,2},{4,5},{5,4},{6,7},{7,6},{8,9},{9,8},{10,11... | collective-permute-start | bytes 184328 | tf_op jit(solution)/shard_map/ppermute | solution.py:488
  23.1 1.0 %pack_donors.1 = (f32[264,128]{1,0:T(8,128)S(1)}, f32[264,128]{1,0:T(8,128)S(1)}, s32[8,128]{1,0:T(8,128)S(1)}) custom-call(f32[8,512,128]{2,1,0:T(8,128)S(1)} %bitcast.6, f32[16,128]{1,0:T(8,128)S(1)} %get-tuple-element.26.own, f32[144,128]{1,0:T(8,128)S(1)} %collective-permute-done.halo_odd, f32[144,128]{1,0:T(8,128)S(1)} %collective-permute-done.1.halo_even, ...), custom_call_target="tpu_custom_call" | custom-call | tf_op jit(solution)/shard_map/pack_donors/pallas_call | solution.py:562
  24.1 5.0 %collective-permute-start.4 = (f32[264,128]{1,0:T(8,128)S(1)}, f32[264,128]{1,0:T(8,128)S(1)}, u32[]{:S(2)}, u32[]{:S(2)}) collective-permute-start(f32[264,128]{1,0:T(8,128)S(1)} %get-tuple-element.34), channel_id=1, source_target_pairs={{16,32},{32,16},{48,64},{64,48},{80,96},{96,80},{112,128},{128,112... | collective-permute-start | bytes 405512 | tf_op jit(solution)/shard_map/ppermute | solution.py:488
  29.1 1.9 %collective-permute-start.5 = (f32[264,128]{1,0:T(8,128)S(1)}, f32[264,128]{1,0:T(8,128)S(1)}, u32[]{:S(2)}, u32[]{:S(2)}) collective-permute-start(f32[264,128]{1,0:T(8,128)S(1)} %get-tuple-element.35), channel_id=1, source_target_pairs={{0,16},{16,0},{32,48},{48,32},{64,80},{80,64},{96,112},{112,96},{1... | collective-permute-start | bytes 405512 | tf_op jit(solution)/shard_map/ppermute | solution.py:488
  31.0 3.6 %step_near.2 = (f32[8,512,128]{2,1,0:T(8,128)S(1)}, f32[16,128]{1,0:T(8,128)S(1)}, f32[512,128]{1,0:T(8,128)S(1)}) custom-call(f32[8,512,128]{2,1,0:T(8,128)S(1)} %bitcast.7, f32[16,128]{1,0:T(8,128)S(1)} %get-tuple-element.26.own, f32[144,128]{1,0:T(8,128)S(1)} %collective-permute-done.halo_odd, f32[144,128]{1,0:T(8,128)S(1)} %collective-permute-done.1.halo_even, ...), custom_call_target="tpu_custom_call" | custom-call | flops 1610612736 | bytes 16777216 | tf_op jit(solution)/shard_map/step_near/pallas_call | solution.py:530
  34.6 3.4 %collective-permute-done.4.donor_odd = f32[264,128]{1,0:T(8,128)S(1)} collective-permute-done((f32[264,128]{1,0:T(8,128)S(1)}, f32[264,128]{1,0:T(8,128)S(1)}, u32[]{:S(2)}, u32[]{:S(2)}) %collective-permute-start.4) | collective-permute-done | bytes 135200 | tf_op jit(solution)/shard_map/ppermute | solution.py:488
  38.1 2.1 %step_one_far.1 = (f32[8,512,128]{2,1,0:T(8,128)S(1)}, f32[136,128]{1,0:T(8,128)S(1)}, f32[136,128]{1,0:T(8,128)S(1)}, f32[264,128]{1,0:T(8,128)S(1)}, f32[264,128]{1,0:T(8,128)S(1)}) custom-call(f32[8,512,128]{2,1,0:T(8,128)S(1)} %get-tuple-element.31.near, f32[16,128]{1,0:T(8,128)S(1)} %get-tuple-element.32.moved.own, ...), custom_call_target="tpu_custom_call" | custom-call | tf_op jit(solution)/shard_map/step_one_far/pallas_call | solution.py:570
  40.2 3.5 %collective-permute-start.6 = (f32[136,128]{1,0:T(8,128)S(1)}, f32[136,128]{1,0:T(8,128)S(1)}, u32[]{:S(2)}, u32[]{:S(2)}) collective-permute-start(f32[136,128]{1,0:T(8,128)S(1)} %get-tuple-element.39), channel_id=1, source_target_pairs={{16,32},{32,16},{48,64},{64,48},{80,96},{96,80},{112,128},{128,112... | collective-permute-start | bytes 208904 | tf_op jit(solution)/shard_map/ppermute | solution.py:488
  43.7 1.9 %collective-permute-start.7 = (f32[136,128]{1,0:T(8,128)S(1)}, f32[136,128]{1,0:T(8,128)S(1)}, u32[]{:S(2)}, u32[]{:S(2)}) collective-permute-start(f32[136,128]{1,0:T(8,128)S(1)} %get-tuple-element.40), channel_id=1, source_target_pairs={{0,16},{16,0},{32,48},{48,32},{64,80},{80,64},{96,112},{112,96},{1... | collective-permute-start | bytes 208904 | tf_op jit(solution)/shard_map/ppermute | solution.py:488
  45.6 6.3 %collective-permute-done.6.halo_odd = f32[136,128]{1,0:T(8,128)S(1)} collective-permute-done((f32[136,128]{1,0:T(8,128)S(1)}, f32[136,128]{1,0:T(8,128)S(1)}, u32[]{:S(2)}, u32[]{:S(2)}) %collective-permute-start.6) | collective-permute-done | bytes 69664 | tf_op jit(solution)/shard_map/ppermute | solution.py:488
  51.9 4.1 %collective-permute-start.8 = (f32[120,128]{1,0:T(8,128)S(1)}, f32[120,128]{1,0:T(8,128)S(1)}, u32[]{:S(2)}, u32[]{:S(2)}) collective-permute-start(f32[120,128]{1,0:T(8,128)S(1)} %get-tuple-element.41), channel_id=1, source_target_pairs={{1,2},{2,1},{3,4},{4,3},{5,6},{6,5},{7,8},{8,7},{9,10},{10,9},{11,... | collective-permute-start | bytes 184328 | tf_op jit(solution)/shard_map/ppermute | solution.py:488
  56.0 3.7 %collective-permute-start.9 = (f32[120,128]{1,0:T(8,128)S(1)}, f32[120,128]{1,0:T(8,128)S(1)}, u32[]{:S(2)}, u32[]{:S(2)}) collective-permute-start(f32[120,128]{1,0:T(8,128)S(1)} %get-tuple-element.42), channel_id=1, source_target_pairs={{0,1},{1,0},{2,3},{3,2},{4,5},{5,4},{6,7},{7,6},{8,9},{9,8},{10,11... | collective-permute-start | bytes 184328 | tf_op jit(solution)/shard_map/ppermute | solution.py:488
  59.7 4.0 %collective-permute-start.10 = (f32[264,128]{1,0:T(8,128)S(1)}, f32[264,128]{1,0:T(8,128)S(1)}, u32[]{:S(2)}, u32[]{:S(2)}) collective-permute-start(f32[264,128]{1,0:T(8,128)S(1)} %get-tuple-element.46), channel_id=1, source_target_pairs={{16,32},{32,16},{48,64},{64,48},{80,96},{96,80},{112,128},{128,112... | collective-permute-start | bytes 405512 | tf_op jit(solution)/shard_map/ppermute | solution.py:488
  63.7 1.9 %collective-permute-start.11 = (f32[264,128]{1,0:T(8,128)S(1)}, f32[264,128]{1,0:T(8,128)S(1)}, u32[]{:S(2)}, u32[]{:S(2)}) collective-permute-start(f32[264,128]{1,0:T(8,128)S(1)} %get-tuple-element.47), channel_id=1, source_target_pairs={{0,16},{16,0},{32,48},{48,32},{64,80},{80,64},{96,112},{112,96},{1... | collective-permute-start | bytes 405512 | tf_op jit(solution)/shard_map/ppermute | solution.py:488
  65.6 3.6 %step_near.3 = (f32[8,512,128]{2,1,0:T(8,128)S(1)}, f32[16,128]{1,0:T(8,128)S(1)}, f32[512,128]{1,0:T(8,128)S(1)}) custom-call(f32[8,512,128]{2,1,0:T(8,128)S(1)} %get-tuple-element.38.density.fields, f32[16,128]{1,0:T(8,128)S(1)} %get-tuple-element.32.moved.own, f32[136,128]{1,0:T(8,128)S(1)} %collective-permute-done.6.halo_odd, ...), custom_call_target="tpu_custom_call" | custom-call | flops 1610612736 | bytes 16777216 | tf_op jit(solution)/shard_map/step_near/pallas_call | solution.py:530
  69.2 6.9 %collective-permute-done.10.donor_odd = f32[264,128]{1,0:T(8,128)S(1)} collective-permute-done((f32[264,128]{1,0:T(8,128)S(1)}, f32[264,128]{1,0:T(8,128)S(1)}, u32[]{:S(2)}, u32[]{:S(2)}) %collective-permute-start.10) | collective-permute-done | bytes 135200 | tf_op jit(solution)/shard_map/ppermute | solution.py:488
  76.1 3.3 %step_two_far.1 = (f32[2,16,32]{2,1,0:T(8,128)}, f32[8,512,128]{2,1,0:T(8,128)}) custom-call(f32[8,512,128]{2,1,0:T(8,128)S(1)} %get-tuple-element.43.near, f32[16,128]{1,0:T(8,128)S(1)} %get-tuple-element.44.moved, f32[512,128]{1,0:T(8,128)S(1)} %get-tuple-element.45.norm, f32[264,128]{1,0:T(8,128)S(1)} %collective-permute-done.10.donor_odd, ...), custom_call_target="tpu_custom_call" | custom-call | tf_op jit(solution)/shard_map/step_two_far/pallas_call | solution.py:583
  (16 shorter events, 0.1 us)
Async XLA Ops:
  0.6 14.3 %copy-start = (f32[8,16,32,128]{3,2,1,0:T(8,128)S(1)}, f32[8,16,32,128]{3,2,1,0:T(8,128)}, u32[]{:S(2)}) copy-start(f32[8,16,32,128]{3,2,1,0:T(8,128)} %param.5) | copy-start | bytes 6291460
  2.3 12.7 %collective-permute-start = (f32[144,128]{1,0:T(8,128)S(1)}, f32[144,128]{1,0:T(8,128)S(1)}, u32[]{:S(2)}, u32[]{:S(2)}) collective-permute-start(f32[144,128]{1,0:T(8,128)S(1)} %get-tuple-element.27), channel_id=1, source_target_pairs={{16,32},{32,16},{48,64},{64,48},{80,96},{96,80},{112,128},{128,112... | collective-permute-start | bytes 221192 | tf_op jit(solution)/shard_map/ppermute | solution.py:488
  9.4 5.6 %collective-permute-start.1 = (f32[144,128]{1,0:T(8,128)S(1)}, f32[144,128]{1,0:T(8,128)S(1)}, u32[]{:S(2)}, u32[]{:S(2)}) collective-permute-start(f32[144,128]{1,0:T(8,128)S(1)} %get-tuple-element.28), channel_id=1, source_target_pairs={{0,16},{16,0},{32,48},{48,32},{64,80},{80,64},{96,112},{112,96},{1... | collective-permute-start | bytes 221192 | tf_op jit(solution)/shard_map/ppermute | solution.py:488
  15.0 16.1 %copy-start.1 = (s32[16,32,4]{1,2,0:T(4,128)S(1)}, s32[16,32,4]{1,2,0:T(4,128)}, u32[]{:S(2)}) copy-start(s32[16,32,4]{1,2,0:T(4,128)} %param.7) | copy-start | bytes 24580
  15.0 16.1 %copy-start.2 = (s32[16,32,4]{1,2,0:T(4,128)S(1)}, s32[16,32,4]{1,2,0:T(4,128)}, u32[]{:S(2)}) copy-start(s32[16,32,4]{1,2,0:T(4,128)} %param.8) | copy-start | bytes 24580
  15.0 16.1 %copy-start.3 = (s32[16,32]{1,0:T(8,128)S(1)}, s32[16,32]{1,0:T(8,128)}, u32[]{:S(2)}) copy-start(s32[16,32]{1,0:T(8,128)} %count.3) | copy-start | bytes 6148
  15.0 16.0 %collective-permute-start.2 = (f32[120,128]{1,0:T(8,128)S(1)}, f32[120,128]{1,0:T(8,128)S(1)}, u32[]{:S(2)}, u32[]{:S(2)}) collective-permute-start(f32[120,128]{1,0:T(8,128)S(1)} %get-tuple-element.29), channel_id=1, source_target_pairs={{1,2},{2,1},{3,4},{4,3},{5,6},{6,5},{7,8},{8,7},{9,10},{10,9},{11,... | collective-permute-start | bytes 184328 | tf_op jit(solution)/shard_map/ppermute | solution.py:488
  18.6 12.4 %collective-permute-start.3 = (f32[120,128]{1,0:T(8,128)S(1)}, f32[120,128]{1,0:T(8,128)S(1)}, u32[]{:S(2)}, u32[]{:S(2)}) collective-permute-start(f32[120,128]{1,0:T(8,128)S(1)} %get-tuple-element.30.after), channel_id=1, source_target_pairs={{0,1},{1,0},{2,3},{3,2},{4,5},{5,4},{6,7},{7,6},{8,9},{9,8},{10,11... | collective-permute-start | bytes 184328 | tf_op jit(solution)/shard_map/ppermute | solution.py:488
  24.1 14.0 %collective-permute-start.4 = (f32[264,128]{1,0:T(8,128)S(1)}, f32[264,128]{1,0:T(8,128)S(1)}, u32[]{:S(2)}, u32[]{:S(2)}) collective-permute-start(f32[264,128]{1,0:T(8,128)S(1)} %get-tuple-element.34), channel_id=1, source_target_pairs={{16,32},{32,16},{48,64},{64,48},{80,96},{96,80},{112,128},{128,112... | collective-permute-start | bytes 405512 | tf_op jit(solution)/shard_map/ppermute | solution.py:488
  29.1 9.0 %collective-permute-start.5 = (f32[264,128]{1,0:T(8,128)S(1)}, f32[264,128]{1,0:T(8,128)S(1)}, u32[]{:S(2)}, u32[]{:S(2)}) collective-permute-start(f32[264,128]{1,0:T(8,128)S(1)} %get-tuple-element.35), channel_id=1, source_target_pairs={{0,16},{16,0},{32,48},{48,32},{64,80},{80,64},{96,112},{112,96},{1... | collective-permute-start | bytes 405512 | tf_op jit(solution)/shard_map/ppermute | solution.py:488
  40.2 11.7 %collective-permute-start.6 = (f32[136,128]{1,0:T(8,128)S(1)}, f32[136,128]{1,0:T(8,128)S(1)}, u32[]{:S(2)}, u32[]{:S(2)}) collective-permute-start(f32[136,128]{1,0:T(8,128)S(1)} %get-tuple-element.39), channel_id=1, source_target_pairs={{16,32},{32,16},{48,64},{64,48},{80,96},{96,80},{112,128},{128,112... | collective-permute-start | bytes 208904 | tf_op jit(solution)/shard_map/ppermute | solution.py:488
  43.7 8.2 %collective-permute-start.7 = (f32[136,128]{1,0:T(8,128)S(1)}, f32[136,128]{1,0:T(8,128)S(1)}, u32[]{:S(2)}, u32[]{:S(2)}) collective-permute-start(f32[136,128]{1,0:T(8,128)S(1)} %get-tuple-element.40), channel_id=1, source_target_pairs={{0,16},{16,0},{32,48},{48,32},{64,80},{80,64},{96,112},{112,96},{1... | collective-permute-start | bytes 208904 | tf_op jit(solution)/shard_map/ppermute | solution.py:488
  51.9 13.7 %collective-permute-start.8 = (f32[120,128]{1,0:T(8,128)S(1)}, f32[120,128]{1,0:T(8,128)S(1)}, u32[]{:S(2)}, u32[]{:S(2)}) collective-permute-start(f32[120,128]{1,0:T(8,128)S(1)} %get-tuple-element.41), channel_id=1, source_target_pairs={{1,2},{2,1},{3,4},{4,3},{5,6},{6,5},{7,8},{8,7},{9,10},{10,9},{11,... | collective-permute-start | bytes 184328 | tf_op jit(solution)/shard_map/ppermute | solution.py:488
  56.0 9.6 %collective-permute-start.9 = (f32[120,128]{1,0:T(8,128)S(1)}, f32[120,128]{1,0:T(8,128)S(1)}, u32[]{:S(2)}, u32[]{:S(2)}) collective-permute-start(f32[120,128]{1,0:T(8,128)S(1)} %get-tuple-element.42), channel_id=1, source_target_pairs={{0,1},{1,0},{2,3},{3,2},{4,5},{5,4},{6,7},{7,6},{8,9},{9,8},{10,11... | collective-permute-start | bytes 184328 | tf_op jit(solution)/shard_map/ppermute | solution.py:488
  59.7 16.4 %collective-permute-start.10 = (f32[264,128]{1,0:T(8,128)S(1)}, f32[264,128]{1,0:T(8,128)S(1)}, u32[]{:S(2)}, u32[]{:S(2)}) collective-permute-start(f32[264,128]{1,0:T(8,128)S(1)} %get-tuple-element.46), channel_id=1, source_target_pairs={{16,32},{32,16},{48,64},{64,48},{80,96},{96,80},{112,128},{128,112... | collective-permute-start | bytes 405512 | tf_op jit(solution)/shard_map/ppermute | solution.py:488
  63.7 12.4 %collective-permute-start.11 = (f32[264,128]{1,0:T(8,128)S(1)}, f32[264,128]{1,0:T(8,128)S(1)}, u32[]{:S(2)}, u32[]{:S(2)}) collective-permute-start(f32[264,128]{1,0:T(8,128)S(1)} %get-tuple-element.47), channel_id=1, source_target_pairs={{0,16},{16,0},{32,48},{48,32},{64,80},{80,64},{96,112},{112,96},{1... | collective-permute-start | bytes 405512 | tf_op jit(solution)/shard_map/ppermute | solution.py:488

commit v3 on v2

--- a/solution.py
+++ b/solution.py
@@ -65,7 +65,7 @@
 
 
 def first_kernel(
-    disp_hbm, fields_hbm, owner_hbm, place_hbm, out_even, out_odd, own, aux, disp, head, tail, owner, place, sems
+    disp_hbm, fields_hbm, owner_hbm, place_hbm, out_even, out_odd, own, aux, slots, disp, head, tail, owner, place, sems
 ):
     tile_x, _, px, _ = parities()
     copies = [
@@ -101,16 +101,19 @@
     code = jnp.where(
         to_left > 0, rank[:CX], jnp.where(to_right > 0, rank[CX:] + CAP, -1.0)
     )
-    aux[:CX, :] = code
     columns = jnp.transpose(jnp.concatenate([code, widen(place[:, 0, :].astype(F32))], axis=0))
     lane = iota((CY, LANES), 1).astype(F32)
+    spot = iota((CY, LANES), 0).astype(F32)
     asked = jnp.zeros((CY, LANES), F32)
+    used = jnp.zeros((CY, LANES), F32)
     for r in range(CX):
-        asked = asked + jnp.where(
-            columns[:CY, r : r + 1] == lane, columns[:CY, CX + r : CX + r + 1], 0.0
-        )
+        hit = columns[:CY, r : r + 1] == lane
+        asked = asked + jnp.where(hit, columns[:CY, CX + r : CX + r + 1], 0.0)
+        used = used + jnp.where(hit, spot + float(r * CY + 1), 0.0)
     request = jnp.broadcast_to(jnp.sum(asked, axis=0, keepdims=True), (8, LANES))
-    aux[CX:, :] = request
+    aux[...] = request
+    used = jnp.broadcast_to(jnp.sum(used, axis=0, keepdims=True), (8, LANES)).astype(jnp.int32)
+    slots[...] = jnp.where(used > 0, used - 1, TILE)
     low, high = head[...], tail[...]
     out_even[:EDGE, :] = pick(px, low, high)
     out_odd[:EDGE, :] = pick(px, high, low)
@@ -181,25 +184,27 @@
     return outs
 
 
-def donor_offsets(own, asked, out_even, out_odd):
-    flat_x, flat_y = flat_rows(own)
+def at_columns(flats, wanted):
     sub = iota((HALF, LANES), 0)
     lane = iota((HALF, LANES), 1)
-    wanted = jnp.sum(
-        jnp.where(sub == lane, jnp.broadcast_to(asked, (HALF, LANES)), 0.0), axis=1, keepdims=True
-    )
-    hit = wanted == iota((HALF, TILE), 1).astype(F32)
-    rows = []
-    for flat in (flat_x, flat_y):
-        column = jnp.sum(jnp.where(hit, flat, 0.0), axis=1, keepdims=True)
-        rows.append(jnp.sum(jnp.where(sub == lane, column, 0.0), axis=0, keepdims=True))
+    column = jnp.sum(
+        jnp.where(sub == lane, jnp.broadcast_to(wanted, (HALF, LANES)), 0.0), axis=1, keepdims=True
+    )
+    hit = column == iota((HALF, TILE), 1).astype(F32)
+    return [jnp.sum(jnp.where(hit, flat, 0.0), axis=1, keepdims=True) for flat in flats]
+
+
+def offset_rows(flats, wanted):
+    diagonal = iota((HALF, LANES), 0) == iota((HALF, LANES), 1)
+    rows = [
+        jnp.sum(jnp.where(diagonal, column, 0.0), axis=0, keepdims=True)
+        for column in at_columns(flats, wanted)
+    ]
     place = iota((8, LANES), 0)
-    even = jnp.where(place == 0, rows[0], jnp.where(place == 1, rows[1], 0.0))
-    out_even[DONOR_ROWS:, :] = even
-    out_odd[DONOR_ROWS:, :] = pltpu.roll(even, LANES - CAP, 1)
-
-
-def donor_kernel(fields, own, halo_odd, halo_even, after, donor_even, donor_odd, asked_out, places, sem):
+    return jnp.where(place == 0, rows[0], jnp.where(place == 1, rows[1], 0.0))
+
+
+def donor_kernel(fields, own, halo_odd, halo_even, donor_even, donor_odd, asked_out, places, sem):
     _, _, px, _ = parities()
     lane = iota((8, LANES), 1)
     even = halo_even[AT_REST:, :]
@@ -212,7 +217,9 @@
     asked_out[...] = asked.astype(jnp.int32)
     copy = pltpu.make_async_copy(asked_out, places, sem)
     copy.start()
-    donor_offsets(own[...], asked[:1], donor_even, donor_odd)
+    offsets = offset_rows(flat_rows(own[...]), asked[:1])
+    donor_even[DONOR_ROWS:, :] = offsets
+    donor_odd[DONOR_ROWS:, :] = pltpu.roll(offsets, LANES - CAP, 1)
     copy.wait()
     take_donors(fields, places, donor_even, donor_odd)
 
@@ -224,7 +231,7 @@
 
 def relax(fields, own, halo_even, halo_odd, y_even, y_odd, dens, ext, mon):
     tile_x, tile_y, px, py = parities()
-    dens[HALO : HALO + CX, SIDE : SIDE + CY, :] = fields[0].reshape(CX, CY, NZ)
+    dens[HALO : HALO + CX, SIDE : SIDE + CY, :] = fields[0, :TILE, :].reshape(CX, CY, NZ)
     left = pick(px, halo_even[:EDGE, :], halo_odd[:EDGE, :])
     right = pick(px, halo_odd[:EDGE, :], halo_even[:EDGE, :])
     dens[:HALO, SIDE : SIDE + CY, :] = left.reshape(HALO, CY, NZ)
@@ -320,7 +327,7 @@
     return at_x, at_y
 
 
-def weigh_near(own, moved, owner, place, count, left_hand, norm):
+def weigh_near(own, moved, owner, place, count, left_hand, norm, inverse):
     tile_x = lax.axis_index("gx")
     flat_x, flat_y = flat_rows(own)
     spot = iota((1, TILE), 1)
@@ -342,126 +349,154 @@
             code = columns[:CY, k * CX + r : k * CX + r + 1]
             total = total + jnp.where(code == spots, dense, 0.0)
         rows = slice(r * CY, (r + 1) * CY)
-        norm[rows, :] = jnp.broadcast_to(jnp.sum(total, axis=1, keepdims=True), (CY, LANES))
+        sums = jnp.broadcast_to(jnp.sum(total, axis=1, keepdims=True), (CY, LANES))
+        norm[rows, :] = sums
+        inverse[rows, :] = jnp.where(sums > 0, 1.0 / sums, 0.0)
         high, low = split(total)
         left_hand[rows, 0:TILE] = high
         left_hand[rows, TILE : 2 * TILE] = low
         left_hand[rows, 2 * TILE : 3 * TILE] = high
 
 
-def weigh_far(moved, aux, even, odd, norm, left_hand, inverse):
+def mix_near(fields, left_hand, right_hand, inverse, out):
+    for f in range(FIELDS):
+        n, lanes = f // 2, slice((f % 2) * NZ, (f % 2) * NZ + NZ)
+        high, low = split(fields[f, :TILE, :])
+        right_hand[n, 0:TILE, lanes] = high
+        right_hand[n, TILE : 2 * TILE, lanes] = high
+        right_hand[n, 2 * TILE : 3 * TILE, lanes] = low
+    for n in range(FIELDS // 2):
+        mixed = jnp.dot(left_hand[...], right_hand[n], preferred_element_type=F32)
+        out[2 * n, :TILE, :] = mixed[:, :NZ] * inverse[...]
+        out[2 * n + 1, :TILE, :] = mixed[:, NZ:] * inverse[...]
+
+
+def near_body(
+    fields, own, halo_odd, halo_even, y_odd, y_even, owner, place, count, slots, asked,
+    near, moved_out, ranked, ranked_norm, ranked_at, next_offsets,
+    dens, ext, mon, left_hand, right_hand, norm, inverse, seats, sem,
+):
+    copy = pltpu.make_async_copy(slots, seats, sem)
+    copy.start()
+    moved = relax(fields, own[...], halo_even, halo_odd, y_even, y_odd, dens, ext, mon)
+    moved_out[...] = moved
+    flats = flat_rows(moved)
+    if asked is not None:
+        next_offsets[...] = offset_rows(flats, asked[:1, :].astype(F32))
+    spot = iota((1, TILE), 1)
+    flats = [flats[0] + (spot // CY).astype(F32), flats[1] + lax.rem(spot, CY).astype(F32)]
+    at_x, at_y = at_columns(flats, slots[:1, :].astype(F32))
+    ranked_at[0] = jnp.broadcast_to(at_x, (HALF, LANES))
+    ranked_at[1] = jnp.broadcast_to(at_y, (HALF, LANES))
+    weigh_near(own[...], moved, owner, place, count, left_hand, norm, inverse)
+    norm[TILE:, :] = jnp.zeros((8, LANES), F32)
+    near[:, TILE:, :] = jnp.zeros((FIELDS, 8, NZ), F32)
+    mix_near(fields, left_hand, right_hand, inverse, near)
+    copy.wait()
+
+    def one(r, carry):
+        seat = seats[0, r]
+        ranked_norm[pl.ds(r, 1), :] = norm[pl.ds(seat, 1), :]
+        for f in range(FIELDS):
+            ranked[f, pl.ds(r, 1), :] = near[f, pl.ds(seat, 1), :]
+        return carry
+
+    lax.fori_loop(0, 2 * CAP, one, 0, unroll=8)
+
+
+def near_kernel_one(*refs):
+    near_body(*refs)
+
+
+def near_kernel_two(*refs):
+    near_body(*refs[:10], None, *refs[10:15], None, *refs[15:])
+
+
+def far_weights(aux, donor_even, donor_odd, ranked_norm, ranked_at):
     _, _, px, _ = parities()
-    request = aux[CX : CX + 1, :].astype(jnp.int32)
+    even, odd = donor_even[DONOR_ROWS:, :], donor_odd[DONOR_ROWS:, :]
+    request = aux[:1, :].astype(jnp.int32)
     lane = iota((1, LANES), 1)
     left = pick(px, even, odd)
     right = pick(px, odd, even)
     far = jnp.where(iota((8, LANES), 1) < CAP, left, pltpu.roll(right, CAP, 1))
     far_x = far[0:1] + jnp.where(lane < CAP, request // CY - CX, request // CY + CX).astype(F32)
     far_y = far[1:2] + lax.rem(request, CY).astype(F32)
-    far_x = jnp.where(lane < HALF, far_x, pltpu.roll(far_x, HALF, 1))
-    far_y = jnp.where(lane < HALF, far_y, pltpu.roll(far_y, HALF, 1))
-    far_lane = lax.rem(lane, HALF).astype(F32)
-    near_half = iota((CY, LANES), 1) < HALF
-    columns = jnp.transpose(aux[...])
-    shifts = jnp.transpose(moved)
-    for r in range(CX):
-        at_x, at_y = placed(shifts, r)
-        code = columns[:CY, r : r + 1]
-        remote = jnp.where(code == far_lane, weight(at_x - far_x, at_y - far_y), 0.0)
-        rows = slice(r * CY, (r + 1) * CY)
-        total = norm[rows, :] + jnp.sum(jnp.where(near_half, remote, 0.0), axis=1, keepdims=True)
-        inverse[rows, :] = 1.0 / total
-        high = remote.astype(BF16).astype(F32)
-        left_hand[rows, :LANES] = jnp.where(near_half, high, remote - high).astype(BF16)
-        left_hand[rows, LANES:] = jnp.where(near_half, high, 0.0).astype(BF16)
-
-
-def mix_near(fields, left_hand, right_hand, out):
-    for f in range(FIELDS):
-        n, lanes = f // 2, slice((f % 2) * NZ, (f % 2) * NZ + NZ)
-        high, low = split(fields[f])
-        right_hand[n, 0:TILE, lanes] = high
-        right_hand[n, TILE : 2 * TILE, lanes] = high
-        right_hand[n, 2 * TILE : 3 * TILE, lanes] = low
-    for n in range(FIELDS // 2):
-        mixed = jnp.dot(left_hand[...], right_hand[n], preferred_element_type=F32)
-        out[2 * n] = mixed[:, :NZ]
-        out[2 * n + 1] = mixed[:, NZ:]
-
-
-def mix_far(near, even, odd, left_hand, right_hand, inverse, out, done=None):
-    _, _, px, _ = parities()
-    for f in range(FIELDS):
-        n, lanes = f // 2, slice((f % 2) * NZ, (f % 2) * NZ + NZ)
-        from_even = even[f * CAP : (f + 1) * CAP, :]
-        from_odd = odd[f * CAP : (f + 1) * CAP, :]
-        left, right = pick(px, from_even, from_odd), pick(px, from_odd, from_even)
-        high, low = split(jnp.concatenate([left, right], axis=0))
-        right_hand[n, 0:HALF, lanes] = high
-        right_hand[n, HALF : 2 * HALF, lanes] = high
-        right_hand[n, 2 * HALF : 3 * HALF, lanes] = low
-        right_hand[n, 3 * HALF :, lanes] = jnp.zeros((HALF, NZ), BF16)
-    for n in range(FIELDS // 2):
-        mixed = jnp.dot(left_hand[...], right_hand[n], preferred_element_type=F32)
-        out[2 * n] = (near[2 * n] + mixed[:, :NZ]) * inverse[...]
-        out[2 * n + 1] = (near[2 * n + 1] + mixed[:, NZ:]) * inverse[...]
-        if done is not None:
-            done(n)
-
-
-def near_kernel(
-    fields, own, halo_odd, halo_even, y_odd, y_even, owner, place, count,
-    near, moved_out, norm,
-    dens, ext, mon, left_hand, right_hand,
-):
-    moved = relax(fields, own[...], halo_even, halo_odd, y_even, y_odd, dens, ext, mon)
-    moved_out[...] = moved
-    weigh_near(own[...], moved, owner, place, count, left_hand, norm)
-    mix_near(fields, left_hand, right_hand, near)
+    diagonal = iota((HALF, LANES), 0) == iota((HALF, LANES), 1)
+    far_x = jnp.sum(jnp.where(diagonal, far_x, 0.0), axis=1, keepdims=True)
+    far_y = jnp.sum(jnp.where(diagonal, far_y, 0.0), axis=1, keepdims=True)
+    far_weight = weight(ranked_at[0] - far_x, ranked_at[1] - far_y)
+    norm = ranked_norm[...]
+    inverse = 1.0 / (norm + far_weight)
+    return norm * inverse, far_weight * inverse
+
+
+def patch(f, near, ranked, shares, donor_even, donor_odd, px, seats, fresh, out):
+    rows = slice(f * CAP, (f + 1) * CAP)
+    even, odd = donor_even[rows, :], donor_odd[rows, :]
+    far = jnp.concatenate([pick(px, even, odd), pick(px, odd, even)], axis=0)
+    fresh[f] = shares[0] * ranked[f] + shares[1] * far
+    out[f] = near[f]
+
+    def one(r, carry):
+        out[f, pl.ds(seats[0, r], 1), :] = fresh[f, pl.ds(r, 1), :]
+        return carry
+
+    lax.fori_loop(0, 2 * CAP, one, 0, unroll=16)
 
 
 def far_kernel(
-    near, moved, norm, donor_odd, donor_even, aux, asked,
-    out, x_even, x_odd, d_even, d_odd,
-    left_hand, right_hand, inverse, places, sem,
+    near, moved, ranked, ranked_norm, ranked_at, donor_odd, donor_even, aux, slots,
+    out, x_even, x_odd,
+    fresh, seats, sem,
 ):
     _, _, px, _ = parities()
-    copy = pltpu.make_async_copy(asked, places, sem)
+    copy = pltpu.make_async_copy(slots, seats, sem)
     copy.start()
-    weigh_far(
-        moved[...], aux, donor_even[DONOR_ROWS:, :], donor_odd[DONOR_ROWS:, :], norm, left_hand, inverse
-    )
-    mix_far(near, donor_even, donor_odd, left_hand, right_hand, inverse, out)
-    low, high = out[0, :EDGE, :], out[0, TILE - EDGE :, :]
+    shares = far_weights(aux, donor_even, donor_odd, ranked_norm, ranked_at)
+    copy.wait()
+    for f in range(FIELDS):
+        patch(f, near, ranked, shares, donor_even, donor_odd, px, seats, fresh, out)
+    low, high = out[0, :EDGE, :], out[0, TILE - EDGE : TILE, :]
     x_even[:EDGE, :] = pick(px, low, high)
     x_odd[:EDGE, :] = pick(px, high, low)
     low, high = moved[:8, :], moved[8:, :]
     x_even[AT_OFFSETS:AT_REST, :] = pick(px, low, high)
     x_odd[AT_OFFSETS:AT_REST, :] = pick(px, high, low)
-    donor_offsets(moved[...], asked[:1, :].astype(F32), d_even, d_odd)
+
+
+def next_donor_kernel(fields, asked, next_offsets, after_odd, after_even, d_even, d_odd, places, sem):
+    copy = pltpu.make_async_copy(asked, places, sem)
+    copy.start()
+    offsets = next_offsets[...]
+    d_even[DONOR_ROWS:, :] = offsets
+    d_odd[DONOR_ROWS:, :] = pltpu.roll(offsets, LANES - CAP, 1)
     copy.wait()
-    take_donors(out, places, d_even, d_odd)
+    take_donors(fields, places, d_even, d_odd)
 
 
 def last_kernel(
-    near, moved, norm, donor_odd, donor_even, aux,
+    near, moved, ranked, ranked_norm, ranked_at, donor_odd, donor_even, aux, slots,
     moved_out, out_hbm,
-    left_hand, right_hand, inverse, out, sems,
+    fresh, seats, out, sem, sems,
 ):
+    _, _, px, _ = parities()
+    copy = pltpu.make_async_copy(slots, seats, sem)
+    copy.start()
     wide = moved[...]
     moved_out[0] = pltpu.roll(wide, LANES - SIDE, 1)[:, :CY]
     moved_out[1] = pltpu.roll(wide, HALF - SIDE, 1)[:, :CY]
-    weigh_far(wide, aux, donor_even[DONOR_ROWS:, :], donor_odd[DONOR_ROWS:, :], norm, left_hand, inverse)
-
-    def copy(n):
-        pair = pl.ds(2 * n, 2)
-        return pltpu.make_async_copy(out.at[pair], out_hbm.at[pair], sems.at[n])
-
-    mix_far(
-        near, donor_even, donor_odd, left_hand, right_hand, inverse, out, lambda n: copy(n).start()
-    )
-    for n in range(FIELDS // 2):
-        copy(n).wait()
+    shares = far_weights(aux, donor_even, donor_odd, ranked_norm, ranked_at)
+    copy.wait()
+
+    def send(f):
+        return pltpu.make_async_copy(out.at[f, pl.ds(0, TILE)], out_hbm.at[f], sems.at[f])
+
+    for f in range(FIELDS):
+        patch(f, near, ranked, shares, donor_even, donor_odd, px, seats, fresh, out)
+        send(f).start()
+    for f in range(FIELDS):
+        send(f).wait()
 
 
 def shape(*dims, dtype=F32):
@@ -502,13 +537,11 @@
     pltpu.VMEM((TILE, 3 * TILE), BF16),
     pltpu.VMEM((FIELDS // 2, 3 * TILE, 2 * NZ), BF16),
 )
-NORM = pltpu.VMEM((TILE, LANES), F32)
-FAR = (
-    pltpu.VMEM((TILE, 4 * HALF), BF16),
-    pltpu.VMEM((FIELDS // 2, 4 * HALF, 2 * NZ), BF16),
-    NORM,
-)
-PLACES = (pltpu.SMEM((8, LANES), jnp.int32), pltpu.SemaphoreType.DMA)
+PADDED = TILE + 8
+NORMS = (pltpu.VMEM((PADDED, LANES), F32), pltpu.VMEM((TILE, LANES), F32))
+SEATS = pltpu.SMEM((8, LANES), jnp.int32)
+PLACES = (SEATS, pltpu.SemaphoreType.DMA)
+FRESH = pltpu.VMEM((FIELDS, HALF, NZ), F32)
 
 
 def whole():
@@ -526,25 +559,30 @@
     )(fields, own, *halo[::-1])
 
 
-def step_near(fields, own, halo, y_halo, owner, place, count):
+def step_near(kernel, *args):
+    outs = (
+        shape(FIELDS, PADDED, NZ), shape(CX, LANES), shape(FIELDS, HALF, NZ), shape(HALF, LANES),
+        shape(2, HALF, LANES), shape(8, LANES),
+    )
     return call(
-        near_kernel,
-        (shape(FIELDS, TILE, NZ), shape(CX, LANES), shape(TILE, LANES)),
-        scratch=RELAX + NEAR,
+        kernel,
+        outs if kernel is near_kernel_one else outs[:5],
+        scratch=RELAX + NEAR + NORMS + PLACES,
         name="step_near",
-        cost=pl.CostEstimate(
+        cost=None if kernel is near_kernel_two else pl.CostEstimate(
             flops=2 * TILE * 3 * TILE * FIELDS * NZ, bytes_accessed=16 << 20, transcendentals=TILE * TILE
         ),
-    )(fields, own, *halo[::-1], *y_halo[::-1], owner, place, count)
+    )(*args)
 
 
 def per_device(fields, displacement, donor_tile, donor_offset, donor_count):
     fields = fields.reshape(FIELDS, TILE, NZ)
     owner = donor_tile.transpose(0, 2, 1)
     place = donor_offset.transpose(0, 2, 1)
-    even, odd, own, aux = call(
+    even, odd, own, aux, slots = call(
         first_kernel,
-        (shape(REQUEST_MSG, LANES), shape(REQUEST_MSG, LANES), shape(CX, LANES), shape(CX + 8, LANES)),
+        (shape(REQUEST_MSG, LANES), shape(REQUEST_MSG, LANES), shape(CX, LANES), shape(8, LANES),
+         shape(8, LANES, dtype=jnp.int32)),
         scratch=(
             pltpu.VMEM((2, CX, CY), F32),
             pltpu.VMEM((EDGE, NZ), F32),
@@ -564,29 +602,42 @@
         (shape(DONOR_MSG, LANES), shape(DONOR_MSG, LANES), shape(8, LANES, dtype=jnp.int32)),
         scratch=PLACES,
         name="pack_donors",
-    )(fields, own, *halo[::-1], y_even)
+    )(fields, own, *halo[::-1])
     donors = swap(d_even, d_odd, "gx")
-    near, own, norm = step_near(fields, own, halo, y_halo, owner, place, donor_count)
-    fields, even, odd, d_even, d_odd = call(
+    plan = (owner, place, donor_count, slots)
+    near, own, ranked, norm, at, offsets = step_near(
+        near_kernel_one, fields, own, *halo[::-1], *y_halo[::-1], *plan, asked
+    )
+    fields, even, odd = call(
         far_kernel,
-        (
-            shape(FIELDS, TILE, NZ), shape(AT_REST, LANES), shape(AT_REST, LANES),
-            shape(DONOR_MSG, LANES), shape(DONOR_MSG, LANES),
-        ),
-        scratch=FAR + PLACES,
+        (shape(FIELDS, PADDED, NZ), shape(AT_REST, LANES), shape(AT_REST, LANES)),
+        scratch=(FRESH,) + PLACES,
         name="step_one_far",
-    )(near, own, norm, *donors[::-1], aux, asked)
+    )(near, own, ranked, norm, at, *donors[::-1], aux, slots)
     halo = swap(even, odd, "gx")
+    donors = swap(
+        *call(
+            next_donor_kernel,
+            (shape(DONOR_MSG, LANES), shape(DONOR_MSG, LANES)),
+            scratch=PLACES,
+            name="pack_next_donors",
+        )(fields, asked, offsets, *halo[::-1]),
+        "gx",
+    )
     y_halo = swap(*columns(fields, own, halo), "gy")
-    donors = swap(d_even, d_odd, "gx")
-    near, own, norm = step_near(fields, own, halo, y_halo, owner, place, donor_count)
+    near, own, ranked, norm, at = step_near(
+        near_kernel_two, fields, own, *halo[::-1], *y_halo[::-1], *plan
+    )
     moved, fields = call(
         last_kernel,
         (shape(2, CX, CY), shape(FIELDS, TILE, NZ)),
-        scratch=FAR + (pltpu.VMEM((FIELDS, TILE, NZ), F32), pltpu.SemaphoreType.DMA((FIELDS // 2,))),
+        scratch=(
+            FRESH, SEATS, pltpu.VMEM((FIELDS, PADDED, NZ), F32),
+            pltpu.SemaphoreType.DMA, pltpu.SemaphoreType.DMA((FIELDS,)),
+        ),
         out_specs=(whole(), pl.BlockSpec(memory_space=pltpu.HBM)),
         name="step_two_far",
-    )(near, own, norm, *donors[::-1], aux)
+    )(near, own, ranked, norm, at, *donors[::-1], aux, slots)
     return moved, fields.reshape(FIELDS, CX, CY, NZ)
 
 

time: 79.8 us -> 82 us (1.028)
  the two profiles are of different devices: /device:TPU:424 before, /device:TPU:158 now
where the time goes in v3:
time: 82 us; the launch traced here: 81.5 us
  starting transfers between devices  59.3 us (72%)
  Pallas kernels  15.4 us (19%)
  waiting for transfers between devices  5.96 us (7%)
  between operations  0.88 us (1%)
    ppermute x12, starting transfers between devices, swap_pairs(): return lax.ppermute(block, axis, route)  59.3 us
    pallas_call x2, Pallas kernels, step_near(): call(kernel, outs if kernel is near_kernel_one else outs[:5], scratch=REL...  7.85 us
    ppermute x12, waiting for transfers between devices, swap_pairs(): return lax.ppermute(block, axis, route)  5.96 us
    pallas_call x1, Pallas kernels, per_device(): call(last_kernel, (shape(2, CX, CY), shape(FIELDS, TILE, NZ)), scratch=(F...  2.71 us
  transfers between devices with their start and end apart: 12, of which 4 were waited for; matrix products, arithmetic and copies ran while one was open for 0% of the time, Pallas kernels for 11%

profile of v3, /device:TPU:158, one launch (start us, length us, event | category | flops | bytes accessed | tf_op | source)
XLA Modules:
  0.0 81.5 jit_solution(13465680986254600951)
XLA Ops:
  0.6 1.6 %pack_first.1 = (f32[144,128]{1,0:T(8,128)S(1)}, f32[144,128]{1,0:T(8,128)S(1)}, f32[16,128]{1,0:T(8,128)S(1)}, f32[8,128]{1,0:T(8,128)S(1)}, s32[8,128]{1,0:T(8,128)S(1)}) custom-call(f32[2,16,32]{2,1,0:T(8,128)} %disp_hbm.1, f32[8,512,128]{2,1,0:T(8,128)} %bitcast.4, s32[16,4,32]{2,1,0:T(4,128)} %bitcast.8, s32[16,4,32]{2,1,0:T(4,128)} %bitcast.11), custom_call_target="tpu_custom_call" | custom-call | tf_op jit(solution)/shard_map/pack_first/pallas_call | solution.py:582
  2.3 2.2 %collective-permute-start = (f32[144,128]{1,0:T(8,128)S(1)}, f32[144,128]{1,0:T(8,128)S(1)}, u32[]{:S(2)}, u32[]{:S(2)}) collective-permute-start(f32[144,128]{1,0:T(8,128)S(1)} %get-tuple-element.33), channel_id=1, source_target_pairs={{16,32},{32,16},{48,64},{64,48},{80,96},{96,80},{112,128},{128,112... | collective-permute-start | bytes 221192 | tf_op jit(solution)/shard_map/ppermute | solution.py:523
  4.4 8.9 %collective-permute-start.1 = (f32[144,128]{1,0:T(8,128)S(1)}, f32[144,128]{1,0:T(8,128)S(1)}, u32[]{:S(2)}, u32[]{:S(2)}) collective-permute-start(f32[144,128]{1,0:T(8,128)S(1)} %get-tuple-element.34), channel_id=1, source_target_pairs={{0,16},{16,0},{32,48},{48,32},{64,80},{80,64},{96,112},{112,96},{1... | collective-permute-start | bytes 221192 | tf_op jit(solution)/shard_map/ppermute | solution.py:523
  13.3 0.0 collective-permute-done.halo_odd.refs_2_
  13.3 0.9 %collective-permute-done.1.halo_even.refs_3_ = f32[144,128]{1,0:T(8,128)S(1)} collective-permute-done((f32[144,128]{1,0:T(8,128)S(1)}, f32[144,128]{1,0:T(8,128)S(1)}, u32[]{:S(2)}, u32[]{:S(2)}) %collective-permute-start.1) | collective-permute-done | bytes 73760 | tf_op jit(solution)/shard_map/ppermute | solution.py:523
  14.3 4.0 %collective-permute-start.2 = (f32[120,128]{1,0:T(8,128)S(1)}, f32[120,128]{1,0:T(8,128)S(1)}, u32[]{:S(2)}, u32[]{:S(2)}) collective-permute-start(f32[120,128]{1,0:T(8,128)S(1)} %get-tuple-element.35), channel_id=1, source_target_pairs={{1,2},{2,1},{3,4},{4,3},{5,6},{6,5},{7,8},{8,7},{9,10},{10,9},{11,... | collective-permute-start | bytes 184328 | tf_op jit(solution)/shard_map/ppermute | solution.py:523
  18.3 1.9 %collective-permute-start.3 = (f32[120,128]{1,0:T(8,128)S(1)}, f32[120,128]{1,0:T(8,128)S(1)}, u32[]{:S(2)}, u32[]{:S(2)}) collective-permute-start(f32[120,128]{1,0:T(8,128)S(1)} %get-tuple-element.36), channel_id=1, source_target_pairs={{0,1},{1,0},{2,3},{3,2},{4,5},{5,4},{6,7},{7,6},{8,9},{9,8},{10,11... | collective-permute-start | bytes 184328 | tf_op jit(solution)/shard_map/ppermute | solution.py:523
  20.2 1.0 %pack_donors.1 = (f32[264,128]{1,0:T(8,128)S(1)}, f32[264,128]{1,0:T(8,128)S(1)}, s32[8,128]{1,0:T(8,128)S(1)}) custom-call(f32[8,512,128]{2,1,0:T(8,128)S(1)} %bitcast.6, f32[16,128]{1,0:T(8,128)S(1)} %get-tuple-element.32.own.refs_1_, f32[144,128]{1,0:T(8,128)S(1)} %collective-permute-done.halo_odd.refs_2_, ...), custom_call_target="tpu_custom_call" | custom-call | tf_op jit(solution)/shard_map/pack_donors/pallas_call | solution.py:600
  21.2 1.9 %collective-permute-start.4 = (f32[264,128]{1,0:T(8,128)S(1)}, f32[264,128]{1,0:T(8,128)S(1)}, u32[]{:S(2)}, u32[]{:S(2)}) collective-permute-start(f32[264,128]{1,0:T(8,128)S(1)} %get-tuple-element.44), channel_id=1, source_target_pairs={{16,32},{32,16},{48,64},{64,48},{80,96},{96,80},{112,128},{128,112... | collective-permute-start | bytes 405512 | tf_op jit(solution)/shard_map/ppermute | solution.py:523
  23.1 10.1 %collective-permute-start.5 = (f32[264,128]{1,0:T(8,128)S(1)}, f32[264,128]{1,0:T(8,128)S(1)}, u32[]{:S(2)}, u32[]{:S(2)}) collective-permute-start(f32[264,128]{1,0:T(8,128)S(1)} %get-tuple-element.45), channel_id=1, source_target_pairs={{0,16},{16,0},{32,48},{48,32},{64,80},{80,64},{96,112},{112,96},{1... | collective-permute-start | bytes 405512 | tf_op jit(solution)/shard_map/ppermute | solution.py:523
  33.3 4.0 %step_near.2 = (f32[8,520,128]{2,1,0:T(8,128)S(1)}, f32[16,128]{1,0:T(8,128)S(1)}, f32[8,64,128]{2,1,0:T(8,128)S(1)}, f32[64,128]{1,0:T(8,128)S(1)}, f32[2,64,128]{2,1,0:T(8,128)S(1)}, /*index=5*/f32[8,128]{1,0:T(8,128)S(1)}) custom-call(f32[8,512,128]{2,1,0:T(8,128)S(1)} %bitcast.7, f32[16,128]{1,0:T(8,128)S(1)} %get-tuple-element.32.own.refs_1_, ...), custom_call_target="tpu_custom_call" | custom-call | flops 1610612736 | bytes 16777216 | tf_op jit(solution)/shard_map/step_near/pallas_call | solution.py:567
  37.3 1.3 %step_one_far.1 = (f32[8,520,128]{2,1,0:T(8,128)S(1)}, f32[136,128]{1,0:T(8,128)S(1)}, f32[136,128]{1,0:T(8,128)S(1)}) custom-call(f32[8,520,128]{2,1,0:T(8,128)S(1)} %get-tuple-element.39.near, f32[16,128]{1,0:T(8,128)S(1)} %get-tuple-element.40.moved.own.refs_1_, f32[8,64,128]{2,1,0:T(8,128)S(1)} %get-tuple-element.41.ranked, ...), custom_call_target="tpu_custom_call" | custom-call | tf_op jit(solution)/shard_map/step_one_far/pallas_call | solution.py:611
  38.6 1.9 %collective-permute-start.6 = (f32[136,128]{1,0:T(8,128)S(1)}, f32[136,128]{1,0:T(8,128)S(1)}, u32[]{:S(2)}, u32[]{:S(2)}) collective-permute-start(f32[136,128]{1,0:T(8,128)S(1)} %get-tuple-element.48), channel_id=1, source_target_pairs={{16,32},{32,16},{48,64},{64,48},{80,96},{96,80},{112,128},{128,112... | collective-permute-start | bytes 208904 | tf_op jit(solution)/shard_map/ppermute | solution.py:523
  40.5 6.7 %collective-permute-start.7 = (f32[136,128]{1,0:T(8,128)S(1)}, f32[136,128]{1,0:T(8,128)S(1)}, u32[]{:S(2)}, u32[]{:S(2)}) collective-permute-start(f32[136,128]{1,0:T(8,128)S(1)} %get-tuple-element.49), channel_id=1, source_target_pairs={{0,16},{16,0},{32,48},{48,32},{64,80},{80,64},{96,112},{112,96},{1... | collective-permute-start | bytes 208904 | tf_op jit(solution)/shard_map/ppermute | solution.py:523
  47.3 0.9 %collective-permute-done.7.halo_even.refs_3_.after_even = f32[136,128]{1,0:T(8,128)S(1)} collective-permute-done((f32[136,128]{1,0:T(8,128)S(1)}, f32[136,128]{1,0:T(8,128)S(1)}, u32[]{:S(2)}, u32[]{:S(2)}) %collective-permute-start.7) | collective-permute-done | bytes 69664 | tf_op jit(solution)/shard_map/ppermute | solution.py:523
  48.2 0.8 %pack_next_donors.1 = (f32[264,128]{1,0:T(8,128)S(1)}, f32[264,128]{1,0:T(8,128)S(1)}) custom-call(f32[8,520,128]{2,1,0:T(8,128)S(1)} %get-tuple-element.47.density.refs_0_.fields, s32[8,128]{1,0:T(8,128)S(1)} %get-tuple-element.38.refs_10_.asked, f32[8,128]{1,0:T(8,128)S(1)} %get-tuple-element.57.next_offsets, ...), custom_call_target="tpu_custom_call" | custom-call | tf_op jit(solution)/shard_map/pack_next_donors/pallas_call | solution.py:619
  49.0 1.9 %collective-permute-start.10 = (f32[264,128]{1,0:T(8,128)S(1)}, f32[264,128]{1,0:T(8,128)S(1)}, u32[]{:S(2)}, u32[]{:S(2)}) collective-permute-start(f32[264,128]{1,0:T(8,128)S(1)} %get-tuple-element.58), channel_id=1, source_target_pairs={{16,32},{32,16},{48,64},{64,48},{80,96},{96,80},{112,128},{128,112... | collective-permute-start | bytes 405512 | tf_op jit(solution)/shard_map/ppermute | solution.py:523
  50.9 8.8 %collective-permute-start.11 = (f32[264,128]{1,0:T(8,128)S(1)}, f32[264,128]{1,0:T(8,128)S(1)}, u32[]{:S(2)}, u32[]{:S(2)}) collective-permute-start(f32[264,128]{1,0:T(8,128)S(1)} %get-tuple-element.59), channel_id=1, source_target_pairs={{0,16},{16,0},{32,48},{48,32},{64,80},{80,64},{96,112},{112,96},{1... | collective-permute-start | bytes 405512 | tf_op jit(solution)/shard_map/ppermute | solution.py:523
  59.8 9.0 %collective-permute-start.8 = (f32[120,128]{1,0:T(8,128)S(1)}, f32[120,128]{1,0:T(8,128)S(1)}, u32[]{:S(2)}, u32[]{:S(2)}) collective-permute-start(f32[120,128]{1,0:T(8,128)S(1)} %get-tuple-element.50), channel_id=1, source_target_pairs={{1,2},{2,1},{3,4},{4,3},{5,6},{6,5},{7,8},{8,7},{9,10},{10,9},{11,... | collective-permute-start | bytes 184328 | tf_op jit(solution)/shard_map/ppermute | solution.py:523
  68.8 1.9 %collective-permute-start.9 = (f32[120,128]{1,0:T(8,128)S(1)}, f32[120,128]{1,0:T(8,128)S(1)}, u32[]{:S(2)}, u32[]{:S(2)}) collective-permute-start(f32[120,128]{1,0:T(8,128)S(1)} %get-tuple-element.51), channel_id=1, source_target_pairs={{0,1},{1,0},{2,3},{3,2},{4,5},{5,4},{6,7},{7,6},{8,9},{9,8},{10,11... | collective-permute-start | bytes 184328 | tf_op jit(solution)/shard_map/ppermute | solution.py:523
  70.7 0.3 collective-permute-done.8.refs_4_
  71.0 3.9 %collective-permute-done.9.refs_5_ = f32[120,128]{1,0:T(8,128)S(1)} collective-permute-done((f32[120,128]{1,0:T(8,128)S(1)}, f32[120,128]{1,0:T(8,128)S(1)}, u32[]{:S(2)}, u32[]{:S(2)}) %collective-permute-start.9) | collective-permute-done | bytes 61472 | tf_op jit(solution)/shard_map/ppermute | solution.py:523
  74.9 3.9 %step_near.3 = (f32[8,520,128]{2,1,0:T(8,128)S(1)}, f32[16,128]{1,0:T(8,128)S(1)}, f32[8,64,128]{2,1,0:T(8,128)S(1)}, f32[64,128]{1,0:T(8,128)S(1)}, f32[2,64,128]{2,1,0:T(8,128)S(1)}) custom-call(f32[8,520,128]{2,1,0:T(8,128)S(1)} %get-tuple-element.47.density.refs_0_.fields, f32[16,128]{1,0:T(8,128)S(1)} %get-tuple-element.40.moved.own.refs_1_, ...), custom_call_target="tpu_custom_call" | custom-call | tf_op jit(solution)/shard_map/step_near/pallas_call | solution.py:567
  78.8 2.7 %step_two_far.1 = (f32[2,16,32]{2,1,0:T(8,128)}, f32[8,512,128]{2,1,0:T(8,128)}) custom-call(f32[8,520,128]{2,1,0:T(8,128)S(1)} %get-tuple-element.52.near, f32[16,128]{1,0:T(8,128)S(1)} %get-tuple-element.53.moved, f32[8,64,128]{2,1,0:T(8,128)S(1)} %get-tuple-element.54.ranked, f32[64,128]{1,0:T(8,128)S(1)} %get-tuple-element.55.ranked_norm, ...), custom_call_target="tpu_custom_call" | custom-call | tf_op jit(solution)/shard_map/step_two_far/pallas_call | solution.py:631
  (17 shorter events, 0.1 us)
Async XLA Ops:
  0.6 13.6 %copy-start = (f32[8,16,32,128]{3,2,1,0:T(8,128)S(1)}, f32[8,16,32,128]{3,2,1,0:T(8,128)}, u32[]{:S(2)}) copy-start(f32[8,16,32,128]{3,2,1,0:T(8,128)} %param.5) | copy-start | bytes 6291460
  2.3 11.1 %collective-permute-start = (f32[144,128]{1,0:T(8,128)S(1)}, f32[144,128]{1,0:T(8,128)S(1)}, u32[]{:S(2)}, u32[]{:S(2)}) collective-permute-start(f32[144,128]{1,0:T(8,128)S(1)} %get-tuple-element.33), channel_id=1, source_target_pairs={{16,32},{32,16},{48,64},{64,48},{80,96},{96,80},{112,128},{128,112... | collective-permute-start | bytes 221192 | tf_op jit(solution)/shard_map/ppermute | solution.py:523
  4.4 9.8 %collective-permute-start.1 = (f32[144,128]{1,0:T(8,128)S(1)}, f32[144,128]{1,0:T(8,128)S(1)}, u32[]{:S(2)}, u32[]{:S(2)}) collective-permute-start(f32[144,128]{1,0:T(8,128)S(1)} %get-tuple-element.34), channel_id=1, source_target_pairs={{0,16},{16,0},{32,48},{48,32},{64,80},{80,64},{96,112},{112,96},{1... | collective-permute-start | bytes 221192 | tf_op jit(solution)/shard_map/ppermute | solution.py:523
  14.2 19.1 %copy-start.1 = (s32[16,32,4]{1,2,0:T(4,128)S(1)}, s32[16,32,4]{1,2,0:T(4,128)}, u32[]{:S(2)}) copy-start(s32[16,32,4]{1,2,0:T(4,128)} %param.7) | copy-start | bytes 24580
  14.2 19.1 %copy-start.2 = (s32[16,32,4]{1,2,0:T(4,128)S(1)}, s32[16,32,4]{1,2,0:T(4,128)}, u32[]{:S(2)}) copy-start(s32[16,32,4]{1,2,0:T(4,128)} %param.8) | copy-start | bytes 24580
  14.2 19.1 %copy-start.3 = (s32[16,32]{1,0:T(8,128)S(1)}, s32[16,32]{1,0:T(8,128)}, u32[]{:S(2)}) copy-start(s32[16,32]{1,0:T(8,128)} %refs_8_.3) | copy-start | bytes 6148
  14.3 19.0 %collective-permute-start.2 = (f32[120,128]{1,0:T(8,128)S(1)}, f32[120,128]{1,0:T(8,128)S(1)}, u32[]{:S(2)}, u32[]{:S(2)}) collective-permute-start(f32[120,128]{1,0:T(8,128)S(1)} %get-tuple-element.35), channel_id=1, source_target_pairs={{1,2},{2,1},{3,4},{4,3},{5,6},{6,5},{7,8},{8,7},{9,10},{10,9},{11,... | collective-permute-start | bytes 184328 | tf_op jit(solution)/shard_map/ppermute | solution.py:523
  18.3 15.0 %collective-permute-start.3 = (f32[120,128]{1,0:T(8,128)S(1)}, f32[120,128]{1,0:T(8,128)S(1)}, u32[]{:S(2)}, u32[]{:S(2)}) collective-permute-start(f32[120,128]{1,0:T(8,128)S(1)} %get-tuple-element.36), channel_id=1, source_target_pairs={{0,1},{1,0},{2,3},{3,2},{4,5},{5,4},{6,7},{7,6},{8,9},{9,8},{10,11... | collective-permute-start | bytes 184328 | tf_op jit(solution)/shard_map/ppermute | solution.py:523
  21.2 16.1 %collective-permute-start.4 = (f32[264,128]{1,0:T(8,128)S(1)}, f32[264,128]{1,0:T(8,128)S(1)}, u32[]{:S(2)}, u32[]{:S(2)}) collective-permute-start(f32[264,128]{1,0:T(8,128)S(1)} %get-tuple-element.44), channel_id=1, source_target_pairs={{16,32},{32,16},{48,64},{64,48},{80,96},{96,80},{112,128},{128,112... | collective-permute-start | bytes 405512 | tf_op jit(solution)/shard_map/ppermute | solution.py:523
  23.1 14.2 %collective-permute-start.5 = (f32[264,128]{1,0:T(8,128)S(1)}, f32[264,128]{1,0:T(8,128)S(1)}, u32[]{:S(2)}, u32[]{:S(2)}) collective-permute-start(f32[264,128]{1,0:T(8,128)S(1)} %get-tuple-element.45), channel_id=1, source_target_pairs={{0,16},{16,0},{32,48},{48,32},{64,80},{80,64},{96,112},{112,96},{1... | collective-permute-start | bytes 405512 | tf_op jit(solution)/shard_map/ppermute | solution.py:523
  38.6 8.7 %collective-permute-start.6 = (f32[136,128]{1,0:T(8,128)S(1)}, f32[136,128]{1,0:T(8,128)S(1)}, u32[]{:S(2)}, u32[]{:S(2)}) collective-permute-start(f32[136,128]{1,0:T(8,128)S(1)} %get-tuple-element.48), channel_id=1, source_target_pairs={{16,32},{32,16},{48,64},{64,48},{80,96},{96,80},{112,128},{128,112... | collective-permute-start | bytes 208904 | tf_op jit(solution)/shard_map/ppermute | solution.py:523
  40.5 7.6 %collective-permute-start.7 = (f32[136,128]{1,0:T(8,128)S(1)}, f32[136,128]{1,0:T(8,128)S(1)}, u32[]{:S(2)}, u32[]{:S(2)}) collective-permute-start(f32[136,128]{1,0:T(8,128)S(1)} %get-tuple-element.49), channel_id=1, source_target_pairs={{0,16},{16,0},{32,48},{48,32},{64,80},{80,64},{96,112},{112,96},{1... | collective-permute-start | bytes 208904 | tf_op jit(solution)/shard_map/ppermute | solution.py:523
  49.0 29.8 %collective-permute-start.10 = (f32[264,128]{1,0:T(8,128)S(1)}, f32[264,128]{1,0:T(8,128)S(1)}, u32[]{:S(2)}, u32[]{:S(2)}) collective-permute-start(f32[264,128]{1,0:T(8,128)S(1)} %get-tuple-element.58), channel_id=1, source_target_pairs={{16,32},{32,16},{48,64},{64,48},{80,96},{96,80},{112,128},{128,112... | collective-permute-start | bytes 405512 | tf_op jit(solution)/shard_map/ppermute | solution.py:523
  50.9 27.9 %collective-permute-start.11 = (f32[264,128]{1,0:T(8,128)S(1)}, f32[264,128]{1,0:T(8,128)S(1)}, u32[]{:S(2)}, u32[]{:S(2)}) collective-permute-start(f32[264,128]{1,0:T(8,128)S(1)} %get-tuple-element.59), channel_id=1, source_target_pairs={{0,16},{16,0},{32,48},{48,32},{64,80},{80,64},{96,112},{112,96},{1... | collective-permute-start | bytes 405512 | tf_op jit(solution)/shard_map/ppermute | solution.py:523
  59.8 11.2 %collective-permute-start.8 = (f32[120,128]{1,0:T(8,128)S(1)}, f32[120,128]{1,0:T(8,128)S(1)}, u32[]{:S(2)}, u32[]{:S(2)}) collective-permute-start(f32[120,128]{1,0:T(8,128)S(1)} %get-tuple-element.50), channel_id=1, source_target_pairs={{1,2},{2,1},{3,4},{4,3},{5,6},{6,5},{7,8},{8,7},{9,10},{10,9},{11,... | collective-permute-start | bytes 184328 | tf_op jit(solution)/shard_map/ppermute | solution.py:523
  68.8 6.1 %collective-permute-start.9 = (f32[120,128]{1,0:T(8,128)S(1)}, f32[120,128]{1,0:T(8,128)S(1)}, u32[]{:S(2)}, u32[]{:S(2)}) collective-permute-start(f32[120,128]{1,0:T(8,128)S(1)} %get-tuple-element.51), channel_id=1, source_target_pairs={{0,1},{1,0},{2,3},{3,2},{4,5},{5,4},{6,7},{7,6},{8,9},{9,8},{10,11... | collective-permute-start | bytes 184328 | tf_op jit(solution)/shard_map/ppermute | solution.py:523
